TPU v7x, 256 devices: a whole 4x4x8 slice. The times are simulated.
256 devices in a mesh: group: 2 (over z_hi), dp: 8 (over x, core), tensor: 16 (over z_lo, y).
Axes of the slice: x: 4, y: 4, z: 8 (z_hi: 2, z_lo: 4; z = z_hi * 4 + z_lo), core: 2. Of those that a mesh axis runs over, the one named last changes fastest.
Arguments:
- teacher_hidden: bfloat16 [4096, 8192], P(('group', 'dp'), 'tensor'), may hold values from -6 to 6
- teacher_gain: float32 [8192], P('tensor'), may hold values from 0.1 to 1.9
- project_weight: bfloat16 [8192, 3584], P('tensor'), may hold values from -0.0625 to 0.0625
- student_hidden: bfloat16 [4096, 3584], P(('group', 'dp', 'tensor')), may hold values from -6 to 6
- student_gain: float32 [3584], replicated, may hold values from 0.1 to 1.9
- gate_weight: bfloat16 [3584, 9472], P(('group', 'dp'), 'tensor'), may hold values from -0.09375 to 0.09375
- up_weight: bfloat16 [3584, 9472], P(('group', 'dp'), 'tensor'), may hold values from -0.09375 to 0.09375
- down_weight: bfloat16 [9472, 3584], P('tensor', ('group', 'dp')), may hold values from -0.0625 to 0.0625
- owner_map: int32 [256, 1], P(('group', 'dp')), may hold values from 0 to 15; in each aligned block of 16 rows (0 to 15, 16 to 31, ...) at most 2 rows name the same one
- token_ids: int32 [4096], P(('group', 'dp', 'tensor')), may hold values from 0 to 511
- token_counts: int32 [256], P(('group', 'dp')), may hold values from 1 to 16
- id_weight: float32 [512], replicated, may hold values from 0.25 to 4
Outputs:
- student_out: bfloat16 [16, 16, 32, 3584], P(('group', 'dp'), 'tensor')
- down_grad: float32 [3584, 9472], P(('group', 'dp'), 'tensor')
Inputs may be any that keep to these rules, and one draw needn't show every extreme that they name: `owner_map`: of the 16 episodes of one index of group and dp (aligned blocks of 16 rows), at most 2 have the same owner; owner o is index o of group and dp in mesh order.
All inputs are finite; a program needn't handle non-finite values.
Results may differ from a plain program's by a relative error of at most 0.02.
Values may be sent and summed in bfloat16 or wider, within the bound.
No kernel may reach another device: no remote copies, remote signals or barrier semaphores. Data moves between devices by JAX's collectives and lax.ppermute only.
A program may use at most 128 MiB of HBM per device.

v0:
```python
import math

import jax
import jax.numpy as jnp
from jax import lax
from jax.experimental import pallas as pl
from jax.experimental.pallas import tpu as pltpu
from jax.sharding import Mesh
from jax.sharding import PartitionSpec as P

DT = 8192
EP_LEN = 16
AXES = {"group": 2, "x": 4, "core": 2, "z": 4, "y": 4}
OWNERS = ("group", "x", "core")
TENSOR = ("z", "y")
EPSILON = 1e-06
F32 = jnp.float32
BF16 = jnp.bfloat16


def shift(array, axis, by):
    size = AXES[axis]
    return lax.ppermute(array, axis, [(i, (i + by) % size) for i in range(size)])


def rolled(array, axis, name):
    doubled = jnp.concatenate([array, array], axis=axis)
    return lax.dynamic_slice_in_dim(doubled, lax.axis_index(name), array.shape[axis], axis)


def unrolled(array, axis, name):
    size = array.shape[axis]
    doubled = jnp.concatenate([array, array], axis=axis)
    return lax.dynamic_slice_in_dim(doubled, size - lax.axis_index(name), size, axis)


def exchange(array, axis, bits):
    return lax.ppermute(array, axis, [(i, i ^ bits) for i in range(AXES[axis])])


def relative_columns(rows):
    n = rows.shape[0]
    blocks = rows.reshape(n, 2, 4, 2, -1).transpose(1, 3, 2, 0, 4)
    blocks = rolled(rolled(rolled(blocks, 0, "group"), 1, "core"), 2, "x")
    return blocks.transpose(3, 0, 1, 2, 4).reshape(n, -1)


def absolute_columns(rows):
    n = rows.shape[0]
    blocks = rows.reshape(n, 2, 2, 4, -1).transpose(1, 2, 3, 0, 4)
    blocks = unrolled(unrolled(unrolled(blocks, 0, "group"), 1, "core"), 2, "x")
    return blocks.transpose(3, 0, 2, 1, 4).reshape(n, -1)


def after(array, *earlier):
    return lax.optimization_barrier((array, *earlier))[0]


def ring_pieces(piece, axis, *gates):
    half = (piece.shape[0] + 31) // 32 * 16
    behind = shift(piece, axis, 1)
    ahead = shift(piece, axis, -1)
    top = shift(after(behind[:half], *gates), axis, 1)
    bottom = shift(after(ahead[half:], *gates), axis, -1)
    return [piece, ahead, top, bottom, behind]


def swapped(pieces):
    return [shift(p, "core", 1) for p in pieces]


def ring_starts(pieces, block, low):
    return [low, low + block, low + 2 * block, low + 2 * block + pieces[2].shape[0], low + 3 * block]


def feed_forward(rows, pieces, starts, hidden):
    tokens, columns = rows.shape[0], pieces[0].shape[1]
    width = sum(p.shape[0] for p in pieces)
    lanes = -(-hidden // 128) * 128
    count, groups = len(pieces), 4
    share = tokens // 4

    def kernel(rows_ref, *refs):
        activated_ref, outs = refs[count], refs[count + 1 : count + 9]
        whole, padded, sems = refs[count + 9 :]
        copies = [
            pltpu.make_async_copy(ref, whole.at[pl.ds(low, ref.shape[0]), :], sems.at[k])
            for k, (ref, low) in enumerate(zip(refs[:count], starts))
        ]
        for c in copies:
            c.start()
        padded[...] = jnp.zeros_like(padded)
        total = None
        for group in range(groups):
            for c in copies[group * count // groups : (group + 1) * count // groups]:
                c.wait()
            span = slice(group * width // groups, (group + 1) * width // groups)
            part = jnp.dot(rows_ref[:, span], whole[span, :], preferred_element_type=F32)
            total = part if total is None else total + part
        gate, up = total[:, hidden : 2 * hidden], total[:, 2 * hidden :]
        activated = (gate / (1.0 + jnp.exp(-gate)) * up).astype(BF16)
        activated_ref[...] = activated
        padded[:, :hidden] = activated
        for k in range(2):
            down = whole[k * width // 2 : (k + 1) * width // 2, :lanes]
            branch = lax.dot_general(
                padded[...], down, (((1,), (1,)), ((), ())), preferred_element_type=F32
            ).astype(BF16)
            for r in range(4):
                outs[4 * k + r][...] = branch[r * share : (r + 1) * share]

    block = jax.ShapeDtypeStruct((share, width // 2), BF16)
    out_shapes = [jax.ShapeDtypeStruct((tokens, hidden), BF16), *[block] * 8]
    activated, *blocks = pl.pallas_call(
        kernel,
        grid=(1,),
        in_specs=[
            pl.BlockSpec(rows.shape, lambda i: (0, 0)),
            *(pl.BlockSpec(memory_space=pltpu.HBM) for _ in pieces),
        ],
        out_specs=[pl.BlockSpec(o.shape, lambda i: (0, 0)) for o in out_shapes],
        out_shape=out_shapes,
        scratch_shapes=[
            pltpu.VMEM((width, columns), BF16),
            pltpu.VMEM((tokens, lanes), BF16),
            pltpu.SemaphoreType.DMA((count,)),
        ],
        compiler_params=pltpu.CompilerParams(vmem_limit_bytes=58 * 2**20),
    )(rows, *pieces)
    return activated, blocks[:4], blocks[4:]


def teacher_parts(rows, gain, weight, positions):
    each = rows.shape[0] // EP_LEN
    share = rows.shape[0] // 4
    sizes = (share, share, share // 2, share // 2, share)

    def kernel(positions_ref, rows_ref, gain_ref, weight_ref, *rest):
        outs, scaled = rest[:-1], rest[-1]
        for k in range(EP_LEN):
            low = pl.multiple_of(positions_ref[k] * each, each)
            wide = rows_ref[pl.ds(low, each), :].astype(F32)
            scaled[k * each : (k + 1) * each, :] = (wide * gain_ref[...]).astype(BF16)
        product = jnp.dot(scaled[...], weight_ref[...], preferred_element_type=F32).astype(BF16)
        low = 0
        for out, size in zip(outs, sizes):
            out[...] = product[low : low + size]
            low += size

    return pl.pallas_call(
        kernel,
        in_specs=[
            pl.BlockSpec(memory_space=pltpu.SMEM),
            *(pl.BlockSpec(memory_space=pltpu.VMEM) for _ in range(3)),
        ],
        out_specs=[pl.BlockSpec(memory_space=pltpu.VMEM) for _ in sizes],
        out_shape=[jax.ShapeDtypeStruct((size, weight.shape[1]), BF16) for size in sizes],
        scratch_shapes=[pltpu.VMEM(rows.shape, BF16)],
        compiler_params=pltpu.CompilerParams(vmem_limit_bytes=40 * 2**20),
    )(positions, rows, gain[None, :], weight)


def gather_z(rows):
    return jnp.concatenate([rows, *(exchange(rows, "z", k) for k in (1, 2, 3))], axis=0)


def added(parts, arrived):
    total = parts.astype(F32)
    for a in arrived:
        total = total + a.astype(F32)
    return total


def scatter_y(blocks):
    return added(blocks[0], [shift(blocks[k], "y", k) for k in (1, 2, 3)])


def scatter_z(parts):
    n = parts.shape[0] // 4
    return added(parts[:n], [exchange(parts[k * n : (k + 1) * n], "z", k) for k in (1, 2, 3)])


def scatter_z_halving(parts, *gates):
    n = parts.shape[0] // 4
    pair = added(parts[: 2 * n], [exchange(parts[2 * n :], "z", 2)])
    return added(pair[:n], [exchange(after(pair[n:].astype(BF16), *gates), "z", 1)])


def scatter_ring(own, first, top, bottom, third, axis, *gates):
    half = top.shape[0]
    top, bottom = shift(top, axis, 1), shift(bottom, axis, -1)
    up = jnp.concatenate([first[:half] + top, first[half:]], axis=0)
    down = jnp.concatenate([third[:half], third[half:] + bottom], axis=0)
    up, down = after(up, *gates), after(down, *gates)
    return added(own, [shift(up, axis, 1), shift(down, axis, -1)]), (top, bottom)


def two_parts(values):
    high = lax.reduce_precision(values, 8, 7)
    both = jnp.concatenate([high, values - high], axis=1).astype(BF16)
    return jnp.pad(both, ((0, 0), (0, 128 - both.shape[1])))


def pick(onehot, rows):
    return jnp.dot(onehot.astype(BF16), rows, preferred_element_type=F32).astype(BF16)


def to_owners(rows, owner_local, gate):
    owner = owner_local[:, 0]
    index = jnp.arange(owner.shape[0], dtype=jnp.int32)
    earlier = (owner[None, :] == owner[:, None]) & (index[None, :] < index[:, None])
    rank = jnp.sum(earlier.astype(jnp.int32), axis=1)
    g, x, c = (lax.axis_index(a) for a in OWNERS)
    to_c = (owner % 2 + c) % 2
    to_g = (owner // 8 + g) % 2
    to_x = (owner // 2 % 4 - x) % 4
    place = (to_g * 4 + to_x) * 2 + rank
    slots = jnp.arange(16, dtype=jnp.int32)[:, None]
    stay = pick((slots == place[None, :]) & (to_c[None, :] == 0), rows)
    leave = pick((slots == place[None, :]) & (to_c[None, :] == 1), rows)
    arrived = shift(leave, "core", 1)
    kept = jnp.concatenate([stay[:8], arrived[:8]], axis=0)
    sent = after(jnp.concatenate([stay[8:], arrived[8:]], axis=0), gate)
    both = jnp.concatenate([kept, shift(sent, "group", 1)], axis=0)
    place = jnp.arange(32, dtype=jnp.int32)
    by_x = pick((place // 2 % 4 * 4 + place // 8) * 2 + place % 2 == place[:, None], both)
    groups = [by_x[8 * k : 8 * (k + 1)] for k in range(4)]
    here = jnp.concatenate([groups[0], *(shift(groups[k], "x", k) for k in (1, 2, 3))], axis=0)
    source = jnp.arange(32, dtype=jnp.int32)
    k, sg, sc, r = source // 8, source // 4 % 2, source // 2 % 2, source % 2
    final = (((g + sg) % 2 * 4 + (x - k) % 4) * 2 + (c + sc) % 2) * 2 + r
    return pick(jnp.arange(32, dtype=jnp.int32)[:, None] == final[None, :], here)


def local(
    teacher_hidden,
    teacher_gain,
    project_weight,
    student_hidden,
    student_gain,
    gate_weight,
    up_weight,
    down_weight,
    owner_map,
    token_ids,
    token_counts,
    id_weight,
):
    episodes = token_counts.shape[0]
    hidden = gate_weight.shape[1]
    width = student_hidden.shape[1]
    block = width // 4
    position = lax.axis_index(TENSOR)
    tokens_all = EP_LEN * episodes * lax.axis_size(OWNERS)

    near = jnp.concatenate([down_weight.T, gate_weight, up_weight], axis=1)
    rows_each = near.shape[0]
    near_far = shift(near, "group", 1)
    near_own = ring_pieces(near, "x")
    near_first, near_last = (near_own[1], near_own[4]), (near_own[2], near_own[3])
    ahead = jnp.arange(EP_LEN, dtype=jnp.int32)
    positions = (lax.axis_index("z") ^ ahead % 4) * 4 + (lax.axis_index("y") + ahead // 4) % 4
    near_across = shift(near, "core", 1)
    rows = after(teacher_hidden, near_across, *near_first)
    parts = teacher_parts(rows, teacher_gain, project_weight, positions)
    near_relayed = [after(p, parts[0]) for p in near_last]
    near_other = [near_across, *swapped([near_own[1], *near_relayed, near_own[4]])]
    student_hidden, teacher_hidden = after(student_hidden, near), after(teacher_hidden, near)
    wide = student_hidden.astype(F32)
    rescale = lax.rsqrt(jnp.mean(wide * wide, axis=1, keepdims=True) + EPSILON)
    normed = (wide * rescale * student_gain[None, :]).astype(BF16)
    both_rows = relative_columns(jnp.concatenate([normed, student_hidden], axis=0))
    student = both_rows[episodes:].astype(F32)
    widened = teacher_hidden.astype(F32)
    squares = jnp.sum(widened * widened, axis=1).reshape(EP_LEN, episodes).T
    column = jnp.concatenate([both_rows[:episodes], two_parts(squares)], axis=1)
    column = after(column, near_far, *near_other)
    pair = jnp.concatenate([column, exchange(column, "z", 1)], axis=0)
    column = jnp.concatenate([pair, exchange(pair, "z", 2)], axis=0)
    far_own = ring_pieces(after(near_far, pair), "x")
    far_first = (far_own[1], far_own[4])
    ahead, top, bottom, behind = far_own[1:]
    far_other = swapped([far_own[0], after(ahead, top, bottom), top, bottom, after(behind, top, bottom)])
    gathered_pieces = ring_pieces(after(column, *far_first, far_other[0]), "y", far_other[1], far_other[4])
    gathered = jnp.concatenate(gathered_pieces, axis=0)
    totals = jnp.sum(gathered[:, width:].reshape(EP_LEN, episodes, -1).astype(F32), axis=0)
    totals = totals[:, :EP_LEN] + totals[:, EP_LEN : 2 * EP_LEN]
    totals = jnp.sum(jnp.where(jnp.arange(EP_LEN)[None, :] == position, totals, 0.0), axis=1)
    inverse = lax.rsqrt(totals / DT + EPSILON)

    total, _ = scatter_ring(*parts, "y")
    total = scatter_z_halving(after(total.astype(BF16), column))
    projected = (total * inverse[:, None]).astype(BF16)
    projected = relative_columns(projected).astype(F32)

    ids = jnp.arange(id_weight.shape[0], dtype=jnp.int32)
    looked = jnp.sum(jnp.where(token_ids[:, None] == ids[None, :], id_weight[None, :], 0.0), axis=1)
    weight = jnp.where(position < token_counts, looked, 0.0).astype(BF16).astype(F32)
    scale = 1.0 / math.sqrt(tokens_all)

    def starts(pieces, low):
        return ring_starts(pieces, rows_each, low) + ring_starts(pieces, rows_each, low + block)

    activated, near_branch, far_branch = feed_forward(
        after(gathered, total),
        near_own + near_other + far_own + far_other,
        starts(near_own, 0) + starts(far_own, 2 * block),
        hidden,
    )

    def gradient_half(far, branch_rows):
        columns = slice(far * 2 * block, (far + 1) * 2 * block)
        predicted = student[:, columns] + scatter_z(branch_rows)
        difference = predicted - projected[:, columns]
        return predicted, gather_z((weight[:, None] * difference * scale).astype(BF16))

    def owners_half(grad):
        mine, other = (
            jnp.einsum(
                "rc,rh->ch", grad[:, a : a + block], activated, preferred_element_type=F32
            ).astype(BF16)
            for a in (0, block)
        )
        both = mine + shift(other, "core", 1)
        quarter = block // 4
        own, first, second, third = (both[k * quarter : (k + 1) * quarter] for k in range(4))
        return own, first, second[: quarter // 2], second[quarter // 2 :], third

    far_rows = scatter_y(far_branch).astype(BF16)
    near_rows = scatter_y(near_branch).astype(BF16)
    far_predicted, far_column = gradient_half(1, far_rows)
    near_predicted, near_column = gradient_half(0, near_rows)
    far_ring, near_ring = ring_pieces(far_column, "y"), ring_pieces(near_column, "y")
    far_grad, near_grad = jnp.concatenate(far_ring, axis=0), jnp.concatenate(near_ring, axis=0)
    far_reduced, far_arrived = scatter_ring(*owners_half(far_grad), "x")
    far_reduced = far_reduced.astype(BF16)
    own, first, top, bottom, third = owners_half(near_grad)
    top, bottom = after(top, *far_arrived), after(bottom, *far_arrived)
    near_reduced, _ = scatter_ring(own, first, top, bottom, third, "x", far_reduced)
    down_grad = near_reduced + shift(far_reduced, "group", 1).astype(F32)

    predicted = [near_predicted, far_predicted]
    rows = jnp.concatenate([p.astype(BF16) for p in predicted], axis=1)
    student_out = to_owners(absolute_columns(rows), owner_map, far_arrived[0])
    return (student_out[None, None], down_grad)


def solution(mesh):
    split = Mesh(mesh.devices.reshape(*AXES.values()), tuple(AXES))
    placed = (
        P(OWNERS, TENSOR),
        P(TENSOR),
        P(TENSOR, None),
        P((*OWNERS, *TENSOR), None),
        P(),
        P(OWNERS, TENSOR),
        P(OWNERS, TENSOR),
        P(TENSOR, OWNERS),
        P(OWNERS, None),
        P((*OWNERS, *TENSOR)),
        P(OWNERS),
        P(),
    )
    return jax.shard_map(
        local,
        mesh=split,
        in_specs=placed,
        out_specs=(P(OWNERS, TENSOR, None, None), P(OWNERS, TENSOR)),
        check_vma=False,
    )
```

profile of v0, /device:TPU:32, one launch (start us, length us, event | category | flops | bytes accessed | tf_op | source)
XLA Modules:
  0.0 248.7 jit_solution(6346511666327143164)
XLA Ops:
  5.1 6.3 %collective-permute-start = (bf16[224,1776]{1,0:T(8,128)(2,1)S(1)}, bf16[224,1776]{1,0:T(8,128)(2,1)}, u32[]{:S(2)}, u32[]{:S(2)}) collective-permute-start(bf16[224,1776]{1,0:T(8,128)(2,1)S(1)} %concatenate.94.refs_0_), channel_id=1, source_target_pairs={{0,128},{128,0},{1,129},{129,1},{2,130},{130,2},{3,131},{131,3},{4... | collective-permute-start | bytes 2386952 | tf_op jit(solution)/shard_map/ppermute | solution.py:23
  17.9 4.3 %collective-permute-done.2.refs_1_ = bf16[224,1776]{1,0:T(8,128)(2,1)S(1)} collective-permute-done((bf16[224,1776]{1,0:T(8,128)(2,1)S(1)}, bf16[224,1776]{1,0:T(8,128)(2,1)S(1)}, u32[]{:S(2)}, u32[]{:S(2)}) %collective-permute-start.2) | collective-permute-done | bytes 795680 | tf_op jit(solution)/shard_map/ppermute | solution.py:23
  22.2 3.4 %collective-permute-done.4.refs_4_ = bf16[224,1776]{1,0:T(8,128)(2,1)S(1)} collective-permute-done((bf16[224,1776]{1,0:T(8,128)(2,1)S(1)}, bf16[224,1776]{1,0:T(8,128)(2,1)S(1)}, u32[]{:S(2)}, u32[]{:S(2)}) %collective-permute-start.4) | collective-permute-done | bytes 795680 | tf_op jit(solution)/shard_map/ppermute | solution.py:23
  35.8 3.3 %collective-permute-start.7 = (bf16[112,1776]{1,0:T(8,128)(2,1)S(1)}, bf16[112,1776]{1,0:T(8,128)(2,1)S(1)}, u32[]{:S(2)}, u32[]{:S(2)}) collective-permute-start(bf16[112,1776]{1,0:T(8,128)(2,1)S(1)} %slice.272), channel_id=1, source_target_pairs={{0,96},{32,0},{64,32},{96,64},{1,97},{33,1},{65,33},{97,65},{2,98}... | collective-permute-start | bytes 1193480 | tf_op jit(solution)/shard_map/ppermute | solution.py:23
  39.9 5.6 %collective-permute-done.5.refs_2_ = bf16[112,1776]{1,0:T(8,128)(2,1)S(1)} collective-permute-done((bf16[112,1776]{1,0:T(8,128)(2,1)S(1)}, bf16[112,1776]{1,0:T(8,128)(2,1)S(1)}, u32[]{:S(2)}, u32[]{:S(2)}) %collective-permute-start.5) | collective-permute-done | bytes 397856 | tf_op jit(solution)/shard_map/ppermute | solution.py:23
  51.9 4.0 %collective-permute-done.10 = bf16[16,3712]{1,0:T(8,128)(2,1)S(1)} collective-permute-done((bf16[16,3712]{1,0:T(8,128)(2,1)S(1)}, bf16[16,3712]{1,0:T(8,128)(2,1)S(1)}, u32[]{:S(2)}, u32[]{:S(2)}) %collective-permute-start.10) | collective-permute-done | bytes 118816 | tf_op jit(solution)/shard_map/ppermute | solution.py:38
  58.7 3.7 %collective-permute-start.12 = (bf16[224,1776]{1,0:T(8,128)(2,1)}, bf16[224,1776]{1,0:T(8,128)(2,1)S(1)}, u32[]{:S(2)}, u32[]{:S(2)}) collective-permute-start(bf16[224,1776]{1,0:T(8,128)(2,1)} %collective-permute-done.refs_10_), channel_id=1, source_target_pairs={{0,96},{32,0},{64,32},{96,64},{1,97},{33,1},{65,33},{97,65},{2,98}... | collective-permute-start | bytes 2386952 | tf_op jit(solution)/shard_map/ppermute | solution.py:23
  62.6 16.9 %collective-permute-done.13.refs_14_ = bf16[224,1776]{1,0:T(8,128)(2,1)S(1)} collective-permute-done((bf16[224,1776]{1,0:T(8,128)(2,1)}, bf16[224,1776]{1,0:T(8,128)(2,1)S(1)}, u32[]{:S(2)}, u32[]{:S(2)}) %collective-permute-start.13) | collective-permute-done | bytes 795680 | tf_op jit(solution)/shard_map/ppermute | solution.py:23
  93.8 3.3 %collective-permute-start.28 = (bf16[16,3584]{1,0:T(8,128)(2,1)S(1)}, bf16[16,3584]{1,0:T(8,128)(2,1)S(1)}, u32[]{:S(2)}, u32[]{:S(2)}) collective-permute-start(bf16[16,3584]{1,0:T(8,128)(2,1)S(1)} %slice.383), channel_id=1, source_target_pairs={{0,4},{4,0},{8,12},{12,8},{1,5},{5,1},{9,13},{13,9},{2,6},{6,2},{1... | collective-permute-start | bytes 344072 | tf_op jit(solution)/shard_map/ppermute | solution.py:38
  98.9 8.9 %collective-permute-start.21 = (bf16[32,3712]{1,0:T(8,128)(2,1)S(1)}, bf16[32,3712]{1,0:T(8,128)(2,1)S(1)}, u32[]{:S(2)}, u32[]{:S(2)}) collective-permute-start(bf16[32,3712]{1,0:T(8,128)(2,1)S(1)} %slice.273), channel_id=1, source_target_pairs={{0,1},{1,2},{2,3},{3,0},{4,5},{5,6},{6,7},{7,4},{8,9},{9,10},{10,1... | collective-permute-start | bytes 712712 | tf_op jit(solution)/shard_map/ppermute | solution.py:23
  107.9 3.3 %collective-permute-start.22 = (bf16[32,3712]{1,0:T(8,128)(2,1)S(1)}, bf16[32,3712]{1,0:T(8,128)(2,1)S(1)}, u32[]{:S(2)}, u32[]{:S(2)}) collective-permute-start(bf16[32,3712]{1,0:T(8,128)(2,1)S(1)} %slice.276), channel_id=1, source_target_pairs={{0,3},{1,0},{2,1},{3,2},{4,7},{5,4},{6,5},{7,6},{8,11},{9,8},{10,9... | collective-permute-start | bytes 712712 | tf_op jit(solution)/shard_map/ppermute | solution.py:23
  111.2 5.6 %collective-permute-done.21 = bf16[32,3712]{1,0:T(8,128)(2,1)S(1)} collective-permute-done((bf16[32,3712]{1,0:T(8,128)(2,1)S(1)}, bf16[32,3712]{1,0:T(8,128)(2,1)S(1)}, u32[]{:S(2)}, u32[]{:S(2)}) %collective-permute-start.21) | collective-permute-done | bytes 237600 | tf_op jit(solution)/shard_map/ppermute | solution.py:23
  118.2 11.3 %shard_map.132 = (bf16[256,592]{1,0:T(8,128)(2,1)}, bf16[64,1792]{1,0:T(8,128)(2,1)}, bf16[64,1792]{1,0:T(8,128)(2,1)}, bf16[64,1792]{1,0:T(8,128)(2,1)}, bf16[6...) custom-call(bf16[256,3712]{1,0:T(8,128)(2,1)} %copy-done.5, ...), custom_call_target="tpu_custom_call" | custom-call | tf_op jit(solution)/shard_map/pallas_call | solution.py:114
  129.6 4.5 %collective-permute-start.38 = (bf16[64,1792]{1,0:T(8,128)(2,1)}, bf16[64,1792]{1,0:T(8,128)(2,1)S(1)}, u32[]{:S(2)}, u32[]{:S(2)}) collective-permute-start(bf16[64,1792]{1,0:T(8,128)(2,1)} %get-tuple-element.60), channel_id=1, source_target_pairs={{0,2},{1,3},{2,0},{3,1},{4,6},{5,7},{6,4},{7,5},{8,10},{9,11},{10,... | collective-permute-start | bytes 688136 | tf_op jit(solution)/shard_map/ppermute | solution.py:23
  136.9 5.1 %collective-permute-done.37 = bf16[64,1792]{1,0:T(8,128)(2,1)S(1)} collective-permute-done((bf16[64,1792]{1,0:T(8,128)(2,1)}, bf16[64,1792]{1,0:T(8,128)(2,1)S(1)}, u32[]{:S(2)}, u32[]{:S(2)}) %collective-permute-start.37) | collective-permute-done | bytes 229408 | tf_op jit(solution)/shard_map/ppermute | solution.py:23
  141.9 3.8 %collective-permute-done.38 = bf16[64,1792]{1,0:T(8,128)(2,1)S(1)} collective-permute-done((bf16[64,1792]{1,0:T(8,128)(2,1)}, bf16[64,1792]{1,0:T(8,128)(2,1)S(1)}, u32[]{:S(2)}, u32[]{:S(2)}) %collective-permute-start.38) | collective-permute-done | bytes 229408 | tf_op jit(solution)/shard_map/ppermute | solution.py:23
  161.8 4.0 %collective-permute-start.57 = (bf16[16,1792]{1,0:T(8,128)(2,1)S(1)}, bf16[16,1792]{1,0:T(8,128)(2,1)S(1)}, u32[]{:S(2)}, u32[]{:S(2)}) collective-permute-start(bf16[16,1792]{1,0:T(8,128)(2,1)S(1)} %get-tuple-element.75), channel_id=1, source_target_pairs={{0,4},{4,0},{8,12},{12,8},{1,5},{5,1},{9,13},{13,9},{2,6},{6,2},{1... | collective-permute-start | bytes 172040 | tf_op jit(solution)/shard_map/ppermute | solution.py:38
  179.3 6.2 %collective-permute-done.61 = bf16[64,1792]{1,0:T(8,128)(2,1)S(1)} collective-permute-done((bf16[64,1792]{1,0:T(8,128)(2,1)S(1)}, bf16[64,1792]{1,0:T(8,128)(2,1)S(1)}, u32[]{:S(2)}, u32[]{:S(2)}) %collective-permute-start.61) | collective-permute-done | bytes 229408 | tf_op jit(solution)/shard_map/ppermute | solution.py:23
  185.7 3.5 %collective-permute-start.63 = (bf16[32,1792]{1,0:T(8,128)(2,1)S(1)}, bf16[32,1792]{1,0:T(8,128)(2,1)S(1)}, u32[]{:S(2)}, u32[]{:S(2)}) collective-permute-start(bf16[32,1792]{1,0:T(8,128)(2,1)S(1)} %slice.307), channel_id=1, source_target_pairs={{0,3},{1,0},{2,1},{3,2},{4,7},{5,4},{6,5},{7,6},{8,11},{9,8},{10,9... | collective-permute-start | bytes 344072 | tf_op jit(solution)/shard_map/ppermute | solution.py:23
  190.6 3.3 %collective-permute-start.50 = (bf16[32,1792]{1,0:T(8,128)(2,1)S(1)}, bf16[32,1792]{1,0:T(8,128)(2,1)S(1)}, u32[]{:S(2)}, u32[]{:S(2)}) collective-permute-start(bf16[32,1792]{1,0:T(8,128)(2,1)S(1)} %slice.297), channel_id=1, source_target_pairs={{0,3},{1,0},{2,1},{3,2},{4,7},{5,4},{6,5},{7,6},{8,11},{9,8},{10,9... | collective-permute-start | bytes 344072 | tf_op jit(solution)/shard_map/ppermute | solution.py:23
  204.6 3.3 %collective-permute-done.52 = bf16[112,592]{0,1:T(8,128)(2,1)S(1)} collective-permute-done((bf16[112,592]{0,1:T(8,128)(2,1)S(1)}, bf16[112,592]{0,1:T(8,128)(2,1)S(1)}, u32[]{:S(2)}, u32[]{:S(2)}) %collective-permute-start.52) | collective-permute-done | bytes 132640 | tf_op jit(solution)/shard_map/ppermute | solution.py:23
  209.8 4.7 %collective-permute-start.53 = (bf16[16,3584]{1,0:T(8,128)(2,1)S(1)}, bf16[16,3584]{1,0:T(8,128)(2,1)S(1)}, u32[]{:S(2)}, u32[]{:S(2)}) collective-permute-start(bf16[16,3584]{1,0:T(8,128)(2,1)S(1)} %pad_maximum_fusion.11), channel_id=1, source_target_pairs={{0,128},{128,0},{1,129},{129,1},{2,130},{130,2},{3,131},{131,3},{4... | collective-permute-start | bytes 344072 | tf_op jit(solution)/shard_map/ppermute | solution.py:23
  230.2 5.0 %collective-permute-start.72 = (bf16[224,592]{0,1:T(8,128)(2,1)S(1)}, bf16[224,592]{0,1:T(8,128)(2,1)S(1)}, u32[]{:S(2)}, u32[]{:S(2)}) collective-permute-start(bf16[224,592]{0,1:T(8,128)(2,1)S(1)} %add_convert_fusion.1), channel_id=1, source_target_pairs={{0,128},{128,0},{1,129},{129,1},{2,130},{130,2},{3,131},{131,3},{4... | collective-permute-start | bytes 795656 | tf_op jit(solution)/shard_map/ppermute | solution.py:23
  242.6 4.7 %collective-permute-done.72 = bf16[224,592]{0,1:T(8,128)(2,1)S(1)} collective-permute-done((bf16[224,592]{0,1:T(8,128)(2,1)S(1)}, bf16[224,592]{0,1:T(8,128)(2,1)S(1)}, u32[]{:S(2)}, u32[]{:S(2)}) %collective-permute-start.72) | collective-permute-done | bytes 265248 | tf_op jit(solution)/shard_map/ppermute | solution.py:23
  (296 shorter events, 118.8 us)
Async XLA Ops:
  2.2 20.0 %collective-permute-start.2 = (bf16[224,1776]{1,0:T(8,128)(2,1)S(1)}, bf16[224,1776]{1,0:T(8,128)(2,1)S(1)}, u32[]{:S(2)}, u32[]{:S(2)}) collective-permute-start(bf16[224,1776]{1,0:T(8,128)(2,1)S(1)} %concatenate.94.refs_0_), channel_id=1, source_target_pairs={{0,96},{32,0},{64,32},{96,64},{1,97},{33,1},{65,33},{97,65},{2,98}... | collective-permute-start | bytes 2386952 | tf_op jit(solution)/shard_map/ppermute | solution.py:23
  5.0 20.6 %collective-permute-start.4 = (bf16[224,1776]{1,0:T(8,128)(2,1)S(1)}, bf16[224,1776]{1,0:T(8,128)(2,1)S(1)}, u32[]{:S(2)}, u32[]{:S(2)}) collective-permute-start(bf16[224,1776]{1,0:T(8,128)(2,1)S(1)} %concatenate.94.refs_0_), channel_id=1, source_target_pairs={{0,32},{32,64},{64,96},{96,0},{1,33},{33,65},{65,97},{97,1},{2,34}... | collective-permute-start | bytes 2386952 | tf_op jit(solution)/shard_map/ppermute | solution.py:23
  5.0 20.6 %collective-permute-start.1 = (bf16[224,1776]{1,0:T(8,128)(2,1)S(1)}, bf16[224,1776]{1,0:T(8,128)(2,1)}, u32[]{:S(2)}, u32[]{:S(2)}) collective-permute-start(bf16[224,1776]{1,0:T(8,128)(2,1)S(1)} %concatenate.94.refs_0_), channel_id=1, source_target_pairs={{0,16},{16,0},{1,17},{17,1},{2,18},{18,2},{3,19},{19,3},{4,20},{20... | collective-permute-start | bytes 2386952 | tf_op jit(solution)/shard_map/ppermute | solution.py:23
  5.1 42.3 %collective-permute-start = (bf16[224,1776]{1,0:T(8,128)(2,1)S(1)}, bf16[224,1776]{1,0:T(8,128)(2,1)}, u32[]{:S(2)}, u32[]{:S(2)}) collective-permute-start(bf16[224,1776]{1,0:T(8,128)(2,1)S(1)} %concatenate.94.refs_0_), channel_id=1, source_target_pairs={{0,128},{128,0},{1,129},{129,1},{2,130},{130,2},{3,131},{131,3},{4... | collective-permute-start | bytes 2386952 | tf_op jit(solution)/shard_map/ppermute | solution.py:23
  47.4 15.0 %collective-permute-start.24 = (bf16[64,3584]{1,0:T(8,128)(2,1)S(1)}, bf16[64,3584]{1,0:T(8,128)(2,1)S(1)}, u32[]{:S(2)}, u32[]{:S(2)}) collective-permute-start(bf16[64,3584]{1,0:T(8,128)(2,1)S(1)} %pad_maximum_fusion), channel_id=1, source_target_pairs={{0,1},{1,2},{2,3},{3,0},{4,5},{5,6},{6,7},{7,4},{8,9},{9,10},{10,1... | collective-permute-start | bytes 1376264 | tf_op jit(solution)/shard_map/ppermute | solution.py:23
  49.2 13.2 %collective-permute-start.26 = (bf16[64,3584]{1,0:T(8,128)(2,1)S(1)}, bf16[64,3584]{1,0:T(8,128)(2,1)S(1)}, u32[]{:S(2)}, u32[]{:S(2)}) collective-permute-start(bf16[64,3584]{1,0:T(8,128)(2,1)S(1)} %pad_maximum_fusion.1), channel_id=1, source_target_pairs={{0,3},{1,0},{2,1},{3,2},{4,7},{5,4},{6,5},{7,6},{8,11},{9,8},{10,9... | collective-permute-start | bytes 1376264 | tf_op jit(solution)/shard_map/ppermute | solution.py:23
  56.6 27.8 %collective-permute-start.11 = (bf16[32,3712]{1,0:T(8,128)(2,1)S(1)}, bf16[32,3712]{1,0:T(8,128)(2,1)S(1)}, u32[]{:S(2)}, u32[]{:S(2)}) collective-permute-start(bf16[32,3712]{1,0:T(8,128)(2,1)S(1)} %get-tuple-element.112), channel_id=1, source_target_pairs={{0,8},{4,12},{8,0},{12,4},{1,9},{5,13},{9,1},{13,5},{2,10},{6,14},... | collective-permute-start | bytes 712712 | tf_op jit(solution)/shard_map/ppermute | solution.py:38
  58.7 20.8 %collective-permute-start.13 = (bf16[224,1776]{1,0:T(8,128)(2,1)}, bf16[224,1776]{1,0:T(8,128)(2,1)S(1)}, u32[]{:S(2)}, u32[]{:S(2)}) collective-permute-start(bf16[224,1776]{1,0:T(8,128)(2,1)} %collective-permute-done.refs_10_), channel_id=1, source_target_pairs={{0,32},{32,64},{64,96},{96,0},{1,33},{33,65},{65,97},{97,1},{2,34}... | collective-permute-start | bytes 2386952 | tf_op jit(solution)/shard_map/ppermute | solution.py:23
  58.7 21.6 %collective-permute-start.12 = (bf16[224,1776]{1,0:T(8,128)(2,1)}, bf16[224,1776]{1,0:T(8,128)(2,1)S(1)}, u32[]{:S(2)}, u32[]{:S(2)}) collective-permute-start(bf16[224,1776]{1,0:T(8,128)(2,1)} %collective-permute-done.refs_10_), channel_id=1, source_target_pairs={{0,96},{32,0},{64,32},{96,64},{1,97},{33,1},{65,33},{97,65},{2,98}... | collective-permute-start | bytes 2386952 | tf_op jit(solution)/shard_map/ppermute | solution.py:23
  62.4 24.0 %collective-permute-start.14 = (bf16[224,1776]{1,0:T(8,128)(2,1)}, bf16[224,1776]{1,0:T(8,128)(2,1)}, u32[]{:S(2)}, u32[]{:S(2)}) collective-permute-start(bf16[224,1776]{1,0:T(8,128)(2,1)} %collective-permute-done.refs_10_), channel_id=1, source_target_pairs={{0,16},{16,0},{1,17},{17,1},{2,18},{18,2},{3,19},{19,3},{4,20},{20... | collective-permute-start | bytes 2386952 | tf_op jit(solution)/shard_map/ppermute | solution.py:23
  93.8 23.4 %collective-permute-start.28 = (bf16[16,3584]{1,0:T(8,128)(2,1)S(1)}, bf16[16,3584]{1,0:T(8,128)(2,1)S(1)}, u32[]{:S(2)}, u32[]{:S(2)}) collective-permute-start(bf16[16,3584]{1,0:T(8,128)(2,1)S(1)} %slice.383), channel_id=1, source_target_pairs={{0,4},{4,0},{8,12},{12,8},{1,5},{5,1},{9,13},{13,9},{2,6},{6,2},{1... | collective-permute-start | bytes 344072 | tf_op jit(solution)/shard_map/ppermute | solution.py:38
  98.1 19.1 %collective-permute-start.29 = (bf16[112,1776]{1,0:T(8,128)(2,1)S(1)}, bf16[112,1776]{1,0:T(8,128)(2,1)S(1)}, u32[]{:S(2)}, u32[]{:S(2)}) collective-permute-start(bf16[112,1776]{1,0:T(8,128)(2,1)S(1)} %copy-done.20), channel_id=1, source_target_pairs={{0,16},{16,0},{1,17},{17,1},{2,18},{18,2},{3,19},{19,3},{4,20},{20... | collective-permute-start | bytes 1193480 | tf_op jit(solution)/shard_map/ppermute | solution.py:23
  98.3 20.0 %collective-permute-start.30 = (bf16[112,1776]{1,0:T(8,128)(2,1)}, bf16[112,1776]{1,0:T(8,128)(2,1)}, u32[]{:S(2)}, u32[]{:S(2)}) collective-permute-start(bf16[112,1776]{1,0:T(8,128)(2,1)} %collective-permute-done.18.refs_13_), channel_id=1, source_target_pairs={{0,16},{16,0},{1,17},{17,1},{2,18},{18,2},{3,19},{19,3},{4,20},{20... | collective-permute-start | bytes 1193480 | tf_op jit(solution)/shard_map/ppermute | solution.py:23
  98.9 17.8 %collective-permute-start.21 = (bf16[32,3712]{1,0:T(8,128)(2,1)S(1)}, bf16[32,3712]{1,0:T(8,128)(2,1)S(1)}, u32[]{:S(2)}, u32[]{:S(2)}) collective-permute-start(bf16[32,3712]{1,0:T(8,128)(2,1)S(1)} %slice.273), channel_id=1, source_target_pairs={{0,1},{1,2},{2,3},{3,0},{4,5},{5,6},{6,7},{7,4},{8,9},{9,10},{10,1... | collective-permute-start | bytes 712712 | tf_op jit(solution)/shard_map/ppermute | solution.py:23
  129.6 16.1 %collective-permute-start.38 = (bf16[64,1792]{1,0:T(8,128)(2,1)}, bf16[64,1792]{1,0:T(8,128)(2,1)S(1)}, u32[]{:S(2)}, u32[]{:S(2)}) collective-permute-start(bf16[64,1792]{1,0:T(8,128)(2,1)} %get-tuple-element.60), channel_id=1, source_target_pairs={{0,2},{1,3},{2,0},{3,1},{4,6},{5,7},{6,4},{7,5},{8,10},{9,11},{10,... | collective-permute-start | bytes 688136 | tf_op jit(solution)/shard_map/ppermute | solution.py:23
  134.1 15.4 %collective-permute-start.31 = (bf16[64,1792]{1,0:T(8,128)(2,1)}, bf16[64,1792]{1,0:T(8,128)(2,1)S(1)}, u32[]{:S(2)}, u32[]{:S(2)}) collective-permute-start(bf16[64,1792]{1,0:T(8,128)(2,1)} %get-tuple-element.55), channel_id=1, source_target_pairs={{0,1},{1,2},{2,3},{3,0},{4,5},{5,6},{6,7},{7,4},{8,9},{9,10},{10,1... | collective-permute-start | bytes 688136 | tf_op jit(solution)/shard_map/ppermute | solution.py:23
  136.2 17.3 %collective-permute-start.32 = (bf16[64,1792]{1,0:T(8,128)(2,1)}, bf16[64,1792]{1,0:T(8,128)(2,1)S(1)}, u32[]{:S(2)}, u32[]{:S(2)}) collective-permute-start(bf16[64,1792]{1,0:T(8,128)(2,1)} %get-tuple-element.56), channel_id=1, source_target_pairs={{0,2},{1,3},{2,0},{3,1},{4,6},{5,7},{6,4},{7,5},{8,10},{9,11},{10,... | collective-permute-start | bytes 688136 | tf_op jit(solution)/shard_map/ppermute | solution.py:23
  174.0 23.3 %collective-permute-start.43 = (bf16[16,3584]{1,0:T(8,128)(2,1)S(1)}, bf16[16,3584]{1,0:T(8,128)(2,1)S(1)}, u32[]{:S(2)}, u32[]{:S(2)}) collective-permute-start(bf16[16,3584]{1,0:T(8,128)(2,1)S(1)} %convolution_convert_fusion.2), channel_id=1, source_target_pairs={{0,16},{16,0},{1,17},{17,1},{2,18},{18,2},{3,19},{19,3},{4,20},{20... | collective-permute-start | bytes 344072 | tf_op jit(solution)/shard_map/ppermute | solution.py:23
  176.7 13.9 %collective-permute-start.47 = (bf16[64,1792]{1,0:T(8,128)(2,1)S(1)}, bf16[64,1792]{1,0:T(8,128)(2,1)S(1)}, u32[]{:S(2)}, u32[]{:S(2)}) collective-permute-start(bf16[64,1792]{1,0:T(8,128)(2,1)S(1)} %pad_maximum_fusion.7), channel_id=1, source_target_pairs={{0,3},{1,0},{2,1},{3,2},{4,7},{5,4},{6,5},{7,6},{8,11},{9,8},{10,9... | collective-permute-start | bytes 688136 | tf_op jit(solution)/shard_map/ppermute | solution.py:23
  208.3 18.4 %collective-permute-start.67 = (bf16[224,592]{0,1:T(8,128)(2,1)S(1)}, bf16[224,592]{0,1:T(8,128)(2,1)S(1)}, u32[]{:S(2)}, u32[]{:S(2)}) collective-permute-start(bf16[224,592]{0,1:T(8,128)(2,1)S(1)} %pad_maximum_fusion.3), channel_id=1, source_target_pairs={{0,32},{32,64},{64,96},{96,0},{1,33},{33,65},{65,97},{97,1},{2,34}... | collective-permute-start | bytes 795656 | tf_op jit(solution)/shard_map/ppermute | solution.py:23
  222.2 15.1 %collective-permute-start.54 = (bf16[8,3584]{1,0:T(8,128)(2,1)S(1)}, bf16[8,3584]{1,0:T(8,128)(2,1)S(1)}, u32[]{:S(2)}, u32[]{:S(2)}) collective-permute-start(bf16[8,3584]{1,0:T(8,128)(2,1)S(1)} %get-tuple-element.103), channel_id=1, source_target_pairs={{0,32},{32,64},{64,96},{96,0},{1,33},{33,65},{65,97},{97,1},{2,34}... | collective-permute-start | bytes 172040 | tf_op jit(solution)/shard_map/ppermute | solution.py:23
  226.9 15.8 %collective-permute-start.69 = (bf16[224,592]{0,1:T(8,128)(2,1)S(1)}, bf16[224,592]{0,1:T(8,128)(2,1)S(1)}, u32[]{:S(2)}, u32[]{:S(2)}) collective-permute-start(bf16[224,592]{0,1:T(8,128)(2,1)S(1)} %pad_maximum_fusion.2), channel_id=1, source_target_pairs={{0,32},{32,64},{64,96},{96,0},{1,33},{33,65},{65,97},{97,1},{2,34}... | collective-permute-start | bytes 795656 | tf_op jit(solution)/shard_map/ppermute | solution.py:23
  228.7 14.0 %collective-permute-start.71 = (bf16[224,592]{0,1:T(8,128)(2,1)S(1)}, bf16[224,592]{0,1:T(8,128)(2,1)S(1)}, u32[]{:S(2)}, u32[]{:S(2)}) collective-permute-start(bf16[224,592]{0,1:T(8,128)(2,1)S(1)} %pad_maximum_fusion.5), channel_id=1, source_target_pairs={{0,96},{32,0},{64,32},{96,64},{1,97},{33,1},{65,33},{97,65},{2,98}... | collective-permute-start | bytes 795656 | tf_op jit(solution)/shard_map/ppermute | solution.py:23
  230.2 17.1 %collective-permute-start.72 = (bf16[224,592]{0,1:T(8,128)(2,1)S(1)}, bf16[224,592]{0,1:T(8,128)(2,1)S(1)}, u32[]{:S(2)}, u32[]{:S(2)}) collective-permute-start(bf16[224,592]{0,1:T(8,128)(2,1)S(1)} %add_convert_fusion.1), channel_id=1, source_target_pairs={{0,128},{128,0},{1,129},{129,1},{2,130},{130,2},{3,131},{131,3},{4... | collective-permute-start | bytes 795656 | tf_op jit(solution)/shard_map/ppermute | solution.py:23
  (76 other events, 728.0 us)
where the time goes:
time: 254 us; the launch traced here: 249 us
  starting transfers between devices  112 us (44%)
  waiting for transfers between devices  90 us (35%)
  local copies, waits for them, and re-layouts  17.1 us (7%)
  Pallas kernels  13 us (5%)
  other arithmetic  11 us (4%)
  matrix products  3.52 us (1%)
    ppermute x57, starting transfers between devices, shift(): lax.ppermute(array, axis, [(i, (i + by) % size) for i in range(size)])  88.6 us
    ppermute x57, waiting for transfers between devices, shift(): lax.ppermute(array, axis, [(i, (i + by) % size) for i in range(size)])  80.1 us
    ppermute x16, starting transfers between devices, exchange(): return lax.ppermute(array, axis, [(i, i ^ bits) for i in range(AXES[axis])])  23.4 us
    pallas_call x1, Pallas kernels, feed_forward(): pl.pallas_call(kernel, grid=(1,), in_specs=[pl.BlockSpec(rows.shape, lamb...  11.3 us
    ppermute x16, waiting for transfers between devices, exchange(): return lax.ppermute(array, axis, [(i, i ^ bits) for i in range(AXES[axis])])  9.91 us
    unnamed x72, local copies, waits for them, and re-layouts  7.2 us
  transfers between devices with their start and end apart: 73, of which 28 were waited for; matrix products, arithmetic and copies ran while one was open for 10% of the time, Pallas kernels for 1%

commit v1 on v0

--- a/solution.py
+++ b/solution.py
@@ -256,15 +256,15 @@
     near = jnp.concatenate([down_weight.T, gate_weight, up_weight], axis=1)
     rows_each = near.shape[0]
     near_far = shift(near, "group", 1)
-    near_own = ring_pieces(near, "x")
-    near_first, near_last = (near_own[1], near_own[4]), (near_own[2], near_own[3])
     ahead = jnp.arange(EP_LEN, dtype=jnp.int32)
     positions = (lax.axis_index("z") ^ ahead % 4) * 4 + (lax.axis_index("y") + ahead // 4) % 4
     near_across = shift(near, "core", 1)
-    rows = after(teacher_hidden, near_across, *near_first)
+    rows = after(teacher_hidden, near_across)
     parts = teacher_parts(rows, teacher_gain, project_weight, positions)
-    near_relayed = [after(p, parts[0]) for p in near_last]
-    near_other = [near_across, *swapped([near_own[1], *near_relayed, near_own[4]])]
+    near_own = ring_pieces(near, "x", parts[0])
+    near_first, near_last = (near_own[1], near_own[4]), (near_own[2], near_own[3])
+    parts = [after(p, *near_first) for p in parts]
+    near_other = [near_across, *swapped(near_own[1:])]
     student_hidden, teacher_hidden = after(student_hidden, near), after(teacher_hidden, near)
     wide = student_hidden.astype(F32)
     rescale = lax.rsqrt(jnp.mean(wide * wide, axis=1, keepdims=True) + EPSILON)

time: 254 us -> 252 us (level)
    ppermute x16, starting transfers between devices: 23.4 us -> 20.6 us  [exchange(): return lax.ppermute(array, axis, [(i, i ^ bits) for i in range(AXES[axis])])]
    unnamed x72 -> x70, local copies, waits for them, and re-layouts: 7.2 us -> 7.31 us
where the time goes in v1:
time: 252 us; the launch traced here: 247 us
  starting transfers between devices  111 us (44%)
  waiting for transfers between devices  89.3 us (35%)
  local copies, waits for them, and re-layouts  17.2 us (7%)
  Pallas kernels  12.9 us (5%)
  other arithmetic  11 us (4%)
  matrix products  3.53 us (1%)
    ppermute x57, starting transfers between devices, shift(): lax.ppermute(array, axis, [(i, (i + by) % size) for i in range(size)])  90.4 us
    ppermute x57, waiting for transfers between devices, shift(): lax.ppermute(array, axis, [(i, (i + by) % size) for i in range(size)])  78.3 us
    ppermute x16, starting transfers between devices, exchange(): return lax.ppermute(array, axis, [(i, i ^ bits) for i in range(AXES[axis])])  20.6 us
    pallas_call x1, Pallas kernels, feed_forward(): pl.pallas_call(kernel, grid=(1,), in_specs=[pl.BlockSpec(rows.shape, lamb...  11.3 us
    ppermute x16, waiting for transfers between devices, exchange(): return lax.ppermute(array, axis, [(i, i ^ bits) for i in range(AXES[axis])])  11 us
    unnamed x70, local copies, waits for them, and re-layouts  7.31 us
  transfers between devices with their start and end apart: 73, of which 28 were waited for; matrix products, arithmetic and copies ran while one was open for 10% of the time, Pallas kernels for 1%

profile of v1, /device:TPU:32, one launch (start us, length us, event | category | flops | bytes accessed | tf_op | source)
XLA Modules:
  0.0 247.1 jit_solution(10127011918953241289)
XLA Ops:
  5.1 6.3 %collective-permute-start = (bf16[224,1776]{1,0:T(8,128)(2,1)S(1)}, bf16[224,1776]{1,0:T(8,128)(2,1)}, u32[]{:S(2)}, u32[]{:S(2)}) collective-permute-start(bf16[224,1776]{1,0:T(8,128)(2,1)S(1)} %concatenate.94.refs_0_), channel_id=1, source_target_pairs={{0,128},{128,0},{1,129},{129,1},{2,130},{130,2},{3,131},{131,3},{4... | collective-permute-start | bytes 2386952 | tf_op jit(solution)/shard_map/ppermute | solution.py:23
  22.9 3.5 %collective-permute-done.4.refs_4_ = bf16[224,1776]{1,0:T(8,128)(2,1)} collective-permute-done((bf16[224,1776]{1,0:T(8,128)(2,1)S(1)}, bf16[224,1776]{1,0:T(8,128)(2,1)}, u32[]{:S(2)}, u32[]{:S(2)}) %collective-permute-start.4) | collective-permute-done | bytes 795680 | tf_op jit(solution)/shard_map/ppermute | solution.py:23
  31.9 3.3 %collective-permute-start.7 = (bf16[112,1776]{1,0:T(8,128)(2,1)S(1)}, bf16[112,1776]{1,0:T(8,128)(2,1)S(1)}, u32[]{:S(2)}, u32[]{:S(2)}) collective-permute-start(bf16[112,1776]{1,0:T(8,128)(2,1)S(1)} %slice.272), channel_id=1, source_target_pairs={{0,96},{32,0},{64,32},{96,64},{1,97},{33,1},{65,33},{97,65},{2,98}... | collective-permute-start | bytes 1193480 | tf_op jit(solution)/shard_map/ppermute | solution.py:23
  35.9 6.2 %collective-permute-done.5.refs_2_ = bf16[112,1776]{1,0:T(8,128)(2,1)S(1)} collective-permute-done((bf16[112,1776]{1,0:T(8,128)(2,1)S(1)}, bf16[112,1776]{1,0:T(8,128)(2,1)S(1)}, u32[]{:S(2)}, u32[]{:S(2)}) %collective-permute-start.5) | collective-permute-done | bytes 397856 | tf_op jit(solution)/shard_map/ppermute | solution.py:23
  42.6 4.5 %collective-permute-done.refs_10_ = bf16[224,1776]{1,0:T(8,128)(2,1)} collective-permute-done((bf16[224,1776]{1,0:T(8,128)(2,1)S(1)}, bf16[224,1776]{1,0:T(8,128)(2,1)}, u32[]{:S(2)}, u32[]{:S(2)}) %collective-permute-start) | collective-permute-done | bytes 795680 | tf_op jit(solution)/shard_map/ppermute | solution.py:23
  51.6 4.0 %collective-permute-done.10 = bf16[16,3712]{1,0:T(8,128)(2,1)S(1)} collective-permute-done((bf16[16,3712]{1,0:T(8,128)(2,1)S(1)}, bf16[16,3712]{1,0:T(8,128)(2,1)S(1)}, u32[]{:S(2)}, u32[]{:S(2)}) %collective-permute-start.10) | collective-permute-done | bytes 118816 | tf_op jit(solution)/shard_map/ppermute | solution.py:38
  60.8 15.4 %collective-permute-done.13.refs_14_ = bf16[224,1776]{1,0:T(8,128)(2,1)S(1)} collective-permute-done((bf16[224,1776]{1,0:T(8,128)(2,1)}, bf16[224,1776]{1,0:T(8,128)(2,1)S(1)}, u32[]{:S(2)}, u32[]{:S(2)}) %collective-permute-start.13) | collective-permute-done | bytes 795680 | tf_op jit(solution)/shard_map/ppermute | solution.py:23
  77.9 3.3 %collective-permute-start.18 = (bf16[112,1776]{1,0:T(8,128)(2,1)}, bf16[112,1776]{1,0:T(8,128)(2,1)}, u32[]{:S(2)}, u32[]{:S(2)}) collective-permute-start(bf16[112,1776]{1,0:T(8,128)(2,1)} %slice.275), channel_id=1, source_target_pairs={{0,96},{32,0},{64,32},{96,64},{1,97},{33,1},{65,33},{97,65},{2,98}... | collective-permute-start | bytes 1193480 | tf_op jit(solution)/shard_map/ppermute | solution.py:23
  87.9 3.5 %collective-permute-done.27 = bf16[32,3584]{1,0:T(8,128)(2,1)S(1)} collective-permute-done((bf16[32,3584]{1,0:T(8,128)(2,1)}, bf16[32,3584]{1,0:T(8,128)(2,1)S(1)}, u32[]{:S(2)}, u32[]{:S(2)}) %collective-permute-start.27) | collective-permute-done | bytes 229408 | tf_op jit(solution)/shard_map/ppermute | solution.py:38
  96.9 8.9 %collective-permute-start.21 = (bf16[32,3712]{1,0:T(8,128)(2,1)S(1)}, bf16[32,3712]{1,0:T(8,128)(2,1)S(1)}, u32[]{:S(2)}, u32[]{:S(2)}) collective-permute-start(bf16[32,3712]{1,0:T(8,128)(2,1)S(1)} %slice.273), channel_id=1, source_target_pairs={{0,1},{1,2},{2,3},{3,0},{4,5},{5,6},{6,7},{7,4},{8,9},{9,10},{10,1... | collective-permute-start | bytes 712712 | tf_op jit(solution)/shard_map/ppermute | solution.py:23
  105.9 3.3 %collective-permute-start.22 = (bf16[32,3712]{1,0:T(8,128)(2,1)S(1)}, bf16[32,3712]{1,0:T(8,128)(2,1)S(1)}, u32[]{:S(2)}, u32[]{:S(2)}) collective-permute-start(bf16[32,3712]{1,0:T(8,128)(2,1)S(1)} %slice.276), channel_id=1, source_target_pairs={{0,3},{1,0},{2,1},{3,2},{4,7},{5,4},{6,5},{7,6},{8,11},{9,8},{10,9... | collective-permute-start | bytes 712712 | tf_op jit(solution)/shard_map/ppermute | solution.py:23
  109.2 6.0 %collective-permute-done.21 = bf16[32,3712]{1,0:T(8,128)(2,1)S(1)} collective-permute-done((bf16[32,3712]{1,0:T(8,128)(2,1)S(1)}, bf16[32,3712]{1,0:T(8,128)(2,1)S(1)}, u32[]{:S(2)}, u32[]{:S(2)}) %collective-permute-start.21) | collective-permute-done | bytes 237600 | tf_op jit(solution)/shard_map/ppermute | solution.py:23
  116.8 11.3 %shard_map.132 = (bf16[256,592]{1,0:T(8,128)(2,1)}, bf16[64,1792]{1,0:T(8,128)(2,1)}, bf16[64,1792]{1,0:T(8,128)(2,1)}, bf16[64,1792]{1,0:T(8,128)(2,1)}, bf16[6...) custom-call(bf16[256,3712]{1,0:T(8,128)(2,1)} %copy-done.5, ...), custom_call_target="tpu_custom_call" | custom-call | tf_op jit(solution)/shard_map/pallas_call | solution.py:114
  128.2 4.5 %collective-permute-start.38 = (bf16[64,1792]{1,0:T(8,128)(2,1)}, bf16[64,1792]{1,0:T(8,128)(2,1)S(1)}, u32[]{:S(2)}, u32[]{:S(2)}) collective-permute-start(bf16[64,1792]{1,0:T(8,128)(2,1)} %get-tuple-element.70), channel_id=1, source_target_pairs={{0,2},{1,3},{2,0},{3,1},{4,6},{5,7},{6,4},{7,5},{8,10},{9,11},{10,... | collective-permute-start | bytes 688136 | tf_op jit(solution)/shard_map/ppermute | solution.py:23
  135.4 6.3 %collective-permute-done.37 = bf16[64,1792]{1,0:T(8,128)(2,1)S(1)} collective-permute-done((bf16[64,1792]{1,0:T(8,128)(2,1)}, bf16[64,1792]{1,0:T(8,128)(2,1)S(1)}, u32[]{:S(2)}, u32[]{:S(2)}) %collective-permute-start.37) | collective-permute-done | bytes 229408 | tf_op jit(solution)/shard_map/ppermute | solution.py:23
  149.0 3.5 %collective-permute-done.32 = bf16[64,1792]{1,0:T(8,128)(2,1)S(1)} collective-permute-done((bf16[64,1792]{1,0:T(8,128)(2,1)}, bf16[64,1792]{1,0:T(8,128)(2,1)S(1)}, u32[]{:S(2)}, u32[]{:S(2)}) %collective-permute-start.32) | collective-permute-done | bytes 229408 | tf_op jit(solution)/shard_map/ppermute | solution.py:23
  173.8 3.3 %collective-permute-start.47 = (bf16[64,1792]{1,0:T(8,128)(2,1)S(1)}, bf16[64,1792]{1,0:T(8,128)(2,1)S(1)}, u32[]{:S(2)}, u32[]{:S(2)}) collective-permute-start(bf16[64,1792]{1,0:T(8,128)(2,1)S(1)} %pad_maximum_fusion.7), channel_id=1, source_target_pairs={{0,3},{1,0},{2,1},{3,2},{4,7},{5,4},{6,5},{7,6},{8,11},{9,8},{10,9... | collective-permute-start | bytes 688136 | tf_op jit(solution)/shard_map/ppermute | solution.py:23
  177.1 6.2 %collective-permute-done.61 = bf16[64,1792]{1,0:T(8,128)(2,1)S(1)} collective-permute-done((bf16[64,1792]{1,0:T(8,128)(2,1)S(1)}, bf16[64,1792]{1,0:T(8,128)(2,1)S(1)}, u32[]{:S(2)}, u32[]{:S(2)}) %collective-permute-start.61) | collective-permute-done | bytes 229408 | tf_op jit(solution)/shard_map/ppermute | solution.py:23
  183.5 3.5 %collective-permute-start.63 = (bf16[32,1792]{1,0:T(8,128)(2,1)S(1)}, bf16[32,1792]{1,0:T(8,128)(2,1)S(1)}, u32[]{:S(2)}, u32[]{:S(2)}) collective-permute-start(bf16[32,1792]{1,0:T(8,128)(2,1)S(1)} %slice.307), channel_id=1, source_target_pairs={{0,3},{1,0},{2,1},{3,2},{4,7},{5,4},{6,5},{7,6},{8,11},{9,8},{10,9... | collective-permute-start | bytes 344072 | tf_op jit(solution)/shard_map/ppermute | solution.py:23
  188.4 3.3 %collective-permute-start.50 = (bf16[32,1792]{1,0:T(8,128)(2,1)S(1)}, bf16[32,1792]{1,0:T(8,128)(2,1)S(1)}, u32[]{:S(2)}, u32[]{:S(2)}) collective-permute-start(bf16[32,1792]{1,0:T(8,128)(2,1)S(1)} %slice.297), channel_id=1, source_target_pairs={{0,3},{1,0},{2,1},{3,2},{4,7},{5,4},{6,5},{7,6},{8,11},{9,8},{10,9... | collective-permute-start | bytes 344072 | tf_op jit(solution)/shard_map/ppermute | solution.py:23
  207.6 5.3 %collective-permute-start.53 = (bf16[16,3584]{1,0:T(8,128)(2,1)S(1)}, bf16[16,3584]{1,0:T(8,128)(2,1)S(1)}, u32[]{:S(2)}, u32[]{:S(2)}) collective-permute-start(bf16[16,3584]{1,0:T(8,128)(2,1)S(1)} %pad_maximum_fusion.11), channel_id=1, source_target_pairs={{0,128},{128,0},{1,129},{129,1},{2,130},{130,2},{3,131},{131,3},{4... | collective-permute-start | bytes 344072 | tf_op jit(solution)/shard_map/ppermute | solution.py:23
  221.5 3.3 %collective-permute-done.70 = bf16[112,592]{0,1:T(8,128)(2,1)S(1)} collective-permute-done((bf16[112,592]{0,1:T(8,128)(2,1)S(1)}, bf16[112,592]{0,1:T(8,128)(2,1)S(1)}, u32[]{:S(2)}, u32[]{:S(2)}) %collective-permute-start.70) | collective-permute-done | bytes 132640 | tf_op jit(solution)/shard_map/ppermute | solution.py:23
  228.5 5.0 %collective-permute-start.72 = (bf16[224,592]{0,1:T(8,128)(2,1)S(1)}, bf16[224,592]{0,1:T(8,128)(2,1)S(1)}, u32[]{:S(2)}, u32[]{:S(2)}) collective-permute-start(bf16[224,592]{0,1:T(8,128)(2,1)S(1)} %add_convert_fusion.1), channel_id=1, source_target_pairs={{0,128},{128,0},{1,129},{129,1},{2,130},{130,2},{3,131},{131,3},{4... | collective-permute-start | bytes 795656 | tf_op jit(solution)/shard_map/ppermute | solution.py:23
  241.0 4.7 %collective-permute-done.72 = bf16[224,592]{0,1:T(8,128)(2,1)S(1)} collective-permute-done((bf16[224,592]{0,1:T(8,128)(2,1)S(1)}, bf16[224,592]{0,1:T(8,128)(2,1)S(1)}, u32[]{:S(2)}, u32[]{:S(2)}) %collective-permute-start.72) | collective-permute-done | bytes 265248 | tf_op jit(solution)/shard_map/ppermute | solution.py:23
  (294 shorter events, 116.7 us)
Async XLA Ops:
  2.2 15.8 %collective-permute-start.1 = (bf16[224,1776]{1,0:T(8,128)(2,1)S(1)}, bf16[224,1776]{1,0:T(8,128)(2,1)S(1)}, u32[]{:S(2)}, u32[]{:S(2)}) collective-permute-start(bf16[224,1776]{1,0:T(8,128)(2,1)S(1)} %concatenate.94.refs_0_), channel_id=1, source_target_pairs={{0,16},{16,0},{1,17},{17,1},{2,18},{18,2},{3,19},{19,3},{4,20},{20... | collective-permute-start | bytes 2386952 | tf_op jit(solution)/shard_map/ppermute | solution.py:23
  2.3 20.6 %collective-permute-start.2 = (bf16[224,1776]{1,0:T(8,128)(2,1)S(1)}, bf16[224,1776]{1,0:T(8,128)(2,1)}, u32[]{:S(2)}, u32[]{:S(2)}) collective-permute-start(bf16[224,1776]{1,0:T(8,128)(2,1)S(1)} %concatenate.94.refs_0_), channel_id=1, source_target_pairs={{0,96},{32,0},{64,32},{96,64},{1,97},{33,1},{65,33},{97,65},{2,98}... | collective-permute-start | bytes 2386952 | tf_op jit(solution)/shard_map/ppermute | solution.py:23
  5.1 21.3 %collective-permute-start.4 = (bf16[224,1776]{1,0:T(8,128)(2,1)S(1)}, bf16[224,1776]{1,0:T(8,128)(2,1)}, u32[]{:S(2)}, u32[]{:S(2)}) collective-permute-start(bf16[224,1776]{1,0:T(8,128)(2,1)S(1)} %concatenate.94.refs_0_), channel_id=1, source_target_pairs={{0,32},{32,64},{64,96},{96,0},{1,33},{33,65},{65,97},{97,1},{2,34}... | collective-permute-start | bytes 2386952 | tf_op jit(solution)/shard_map/ppermute | solution.py:23
  5.1 42.0 %collective-permute-start = (bf16[224,1776]{1,0:T(8,128)(2,1)S(1)}, bf16[224,1776]{1,0:T(8,128)(2,1)}, u32[]{:S(2)}, u32[]{:S(2)}) collective-permute-start(bf16[224,1776]{1,0:T(8,128)(2,1)S(1)} %concatenate.94.refs_0_), channel_id=1, source_target_pairs={{0,128},{128,0},{1,129},{129,1},{2,130},{130,2},{3,131},{131,3},{4... | collective-permute-start | bytes 2386952 | tf_op jit(solution)/shard_map/ppermute | solution.py:23
  35.2 15.5 %collective-permute-start.3 = (bf16[224,1776]{1,0:T(8,128)(2,1)}, bf16[224,1776]{1,0:T(8,128)(2,1)S(1)}, u32[]{:S(2)}, u32[]{:S(2)}) collective-permute-start(bf16[224,1776]{1,0:T(8,128)(2,1)} %collective-permute-done.2.refs_1_), channel_id=1, source_target_pairs={{0,16},{16,0},{1,17},{17,1},{2,18},{18,2},{3,19},{19,3},{4,20},{20... | collective-permute-start | bytes 2386952 | tf_op jit(solution)/shard_map/ppermute | solution.py:23
  35.2 15.5 %collective-permute-start.9 = (bf16[224,1776]{1,0:T(8,128)(2,1)}, bf16[224,1776]{1,0:T(8,128)(2,1)S(1)}, u32[]{:S(2)}, u32[]{:S(2)}) collective-permute-start(bf16[224,1776]{1,0:T(8,128)(2,1)} %collective-permute-done.4.refs_4_), channel_id=1, source_target_pairs={{0,16},{16,0},{1,17},{17,1},{2,18},{18,2},{3,19},{19,3},{4,20},{20... | collective-permute-start | bytes 2386952 | tf_op jit(solution)/shard_map/ppermute | solution.py:23
  56.3 24.9 %collective-permute-start.11 = (bf16[32,3712]{1,0:T(8,128)(2,1)S(1)}, bf16[32,3712]{1,0:T(8,128)(2,1)S(1)}, u32[]{:S(2)}, u32[]{:S(2)}) collective-permute-start(bf16[32,3712]{1,0:T(8,128)(2,1)S(1)} %get-tuple-element.122), channel_id=1, source_target_pairs={{0,8},{4,12},{8,0},{12,4},{1,9},{5,13},{9,1},{13,5},{2,10},{6,14},... | collective-permute-start | bytes 712712 | tf_op jit(solution)/shard_map/ppermute | solution.py:38
  57.0 19.2 %collective-permute-start.13 = (bf16[224,1776]{1,0:T(8,128)(2,1)}, bf16[224,1776]{1,0:T(8,128)(2,1)S(1)}, u32[]{:S(2)}, u32[]{:S(2)}) collective-permute-start(bf16[224,1776]{1,0:T(8,128)(2,1)} %collective-permute-done.refs_10_), channel_id=1, source_target_pairs={{0,32},{32,64},{64,96},{96,0},{1,33},{33,65},{65,97},{97,1},{2,34}... | collective-permute-start | bytes 2386952 | tf_op jit(solution)/shard_map/ppermute | solution.py:23
  57.5 19.5 %collective-permute-start.12 = (bf16[224,1776]{1,0:T(8,128)(2,1)}, bf16[224,1776]{1,0:T(8,128)(2,1)S(1)}, u32[]{:S(2)}, u32[]{:S(2)}) collective-permute-start(bf16[224,1776]{1,0:T(8,128)(2,1)} %collective-permute-done.refs_10_), channel_id=1, source_target_pairs={{0,96},{32,0},{64,32},{96,64},{1,97},{33,1},{65,33},{97,65},{2,98}... | collective-permute-start | bytes 2386952 | tf_op jit(solution)/shard_map/ppermute | solution.py:23
  60.5 24.5 %collective-permute-start.14 = (bf16[224,1776]{1,0:T(8,128)(2,1)}, bf16[224,1776]{1,0:T(8,128)(2,1)}, u32[]{:S(2)}, u32[]{:S(2)}) collective-permute-start(bf16[224,1776]{1,0:T(8,128)(2,1)} %collective-permute-done.refs_10_), channel_id=1, source_target_pairs={{0,16},{16,0},{1,17},{17,1},{2,18},{18,2},{3,19},{19,3},{4,20},{20... | collective-permute-start | bytes 2386952 | tf_op jit(solution)/shard_map/ppermute | solution.py:23
  91.5 24.1 %collective-permute-start.28 = (bf16[16,3584]{1,0:T(8,128)(2,1)S(1)}, bf16[16,3584]{1,0:T(8,128)(2,1)S(1)}, u32[]{:S(2)}, u32[]{:S(2)}) collective-permute-start(bf16[16,3584]{1,0:T(8,128)(2,1)S(1)} %slice.383), channel_id=1, source_target_pairs={{0,4},{4,0},{8,12},{12,8},{1,5},{5,1},{9,13},{13,9},{2,6},{6,2},{1... | collective-permute-start | bytes 344072 | tf_op jit(solution)/shard_map/ppermute | solution.py:38
  95.3 20.4 %collective-permute-start.29 = (bf16[112,1776]{1,0:T(8,128)(2,1)S(1)}, bf16[112,1776]{1,0:T(8,128)(2,1)S(1)}, u32[]{:S(2)}, u32[]{:S(2)}) collective-permute-start(bf16[112,1776]{1,0:T(8,128)(2,1)S(1)} %copy-done.19), channel_id=1, source_target_pairs={{0,16},{16,0},{1,17},{17,1},{2,18},{18,2},{3,19},{19,3},{4,20},{20... | collective-permute-start | bytes 1193480 | tf_op jit(solution)/shard_map/ppermute | solution.py:23
  96.9 19.9 %collective-permute-start.30 = (bf16[112,1776]{1,0:T(8,128)(2,1)}, bf16[112,1776]{1,0:T(8,128)(2,1)}, u32[]{:S(2)}, u32[]{:S(2)}) collective-permute-start(bf16[112,1776]{1,0:T(8,128)(2,1)} %collective-permute-done.18.refs_13_), channel_id=1, source_target_pairs={{0,16},{16,0},{1,17},{17,1},{2,18},{18,2},{3,19},{19,3},{4,20},{20... | collective-permute-start | bytes 1193480 | tf_op jit(solution)/shard_map/ppermute | solution.py:23
  96.9 18.3 %collective-permute-start.21 = (bf16[32,3712]{1,0:T(8,128)(2,1)S(1)}, bf16[32,3712]{1,0:T(8,128)(2,1)S(1)}, u32[]{:S(2)}, u32[]{:S(2)}) collective-permute-start(bf16[32,3712]{1,0:T(8,128)(2,1)S(1)} %slice.273), channel_id=1, source_target_pairs={{0,1},{1,2},{2,3},{3,0},{4,5},{5,6},{6,7},{7,4},{8,9},{9,10},{10,1... | collective-permute-start | bytes 712712 | tf_op jit(solution)/shard_map/ppermute | solution.py:23
  128.2 16.2 %collective-permute-start.38 = (bf16[64,1792]{1,0:T(8,128)(2,1)}, bf16[64,1792]{1,0:T(8,128)(2,1)S(1)}, u32[]{:S(2)}, u32[]{:S(2)}) collective-permute-start(bf16[64,1792]{1,0:T(8,128)(2,1)} %get-tuple-element.70), channel_id=1, source_target_pairs={{0,2},{1,3},{2,0},{3,1},{4,6},{5,7},{6,4},{7,5},{8,10},{9,11},{10,... | collective-permute-start | bytes 688136 | tf_op jit(solution)/shard_map/ppermute | solution.py:23
  132.6 15.4 %collective-permute-start.31 = (bf16[64,1792]{1,0:T(8,128)(2,1)}, bf16[64,1792]{1,0:T(8,128)(2,1)S(1)}, u32[]{:S(2)}, u32[]{:S(2)}) collective-permute-start(bf16[64,1792]{1,0:T(8,128)(2,1)} %get-tuple-element.65), channel_id=1, source_target_pairs={{0,1},{1,2},{2,3},{3,0},{4,5},{5,6},{6,7},{7,4},{8,9},{9,10},{10,1... | collective-permute-start | bytes 688136 | tf_op jit(solution)/shard_map/ppermute | solution.py:23
  134.7 17.9 %collective-permute-start.32 = (bf16[64,1792]{1,0:T(8,128)(2,1)}, bf16[64,1792]{1,0:T(8,128)(2,1)S(1)}, u32[]{:S(2)}, u32[]{:S(2)}) collective-permute-start(bf16[64,1792]{1,0:T(8,128)(2,1)} %get-tuple-element.66), channel_id=1, source_target_pairs={{0,2},{1,3},{2,0},{3,1},{4,6},{5,7},{6,4},{7,5},{8,10},{9,11},{10,... | collective-permute-start | bytes 688136 | tf_op jit(solution)/shard_map/ppermute | solution.py:23
  170.4 24.6 %collective-permute-start.43 = (bf16[16,3584]{1,0:T(8,128)(2,1)S(1)}, bf16[16,3584]{1,0:T(8,128)(2,1)S(1)}, u32[]{:S(2)}, u32[]{:S(2)}) collective-permute-start(bf16[16,3584]{1,0:T(8,128)(2,1)S(1)} %convolution_convert_fusion.2), channel_id=1, source_target_pairs={{0,16},{16,0},{1,17},{17,1},{2,18},{18,2},{3,19},{19,3},{4,20},{20... | collective-permute-start | bytes 344072 | tf_op jit(solution)/shard_map/ppermute | solution.py:23
  173.8 14.6 %collective-permute-start.47 = (bf16[64,1792]{1,0:T(8,128)(2,1)S(1)}, bf16[64,1792]{1,0:T(8,128)(2,1)S(1)}, u32[]{:S(2)}, u32[]{:S(2)}) collective-permute-start(bf16[64,1792]{1,0:T(8,128)(2,1)S(1)} %pad_maximum_fusion.7), channel_id=1, source_target_pairs={{0,3},{1,0},{2,1},{3,2},{4,7},{5,4},{6,5},{7,6},{8,11},{9,8},{10,9... | collective-permute-start | bytes 688136 | tf_op jit(solution)/shard_map/ppermute | solution.py:23
  206.1 19.0 %collective-permute-start.67 = (bf16[224,592]{0,1:T(8,128)(2,1)S(1)}, bf16[224,592]{0,1:T(8,128)(2,1)S(1)}, u32[]{:S(2)}, u32[]{:S(2)}) collective-permute-start(bf16[224,592]{0,1:T(8,128)(2,1)S(1)} %pad_maximum_fusion.3), channel_id=1, source_target_pairs={{0,32},{32,64},{64,96},{96,0},{1,33},{33,65},{65,97},{97,1},{2,34}... | collective-permute-start | bytes 795656 | tf_op jit(solution)/shard_map/ppermute | solution.py:23
  220.0 15.7 %collective-permute-start.54 = (bf16[8,3584]{1,0:T(8,128)(2,1)S(1)}, bf16[8,3584]{1,0:T(8,128)(2,1)S(1)}, u32[]{:S(2)}, u32[]{:S(2)}) collective-permute-start(bf16[8,3584]{1,0:T(8,128)(2,1)S(1)} %get-tuple-element.113), channel_id=1, source_target_pairs={{0,32},{32,64},{64,96},{96,0},{1,33},{33,65},{65,97},{97,1},{2,34}... | collective-permute-start | bytes 172040 | tf_op jit(solution)/shard_map/ppermute | solution.py:23
  225.2 15.8 %collective-permute-start.69 = (bf16[224,592]{0,1:T(8,128)(2,1)S(1)}, bf16[224,592]{0,1:T(8,128)(2,1)S(1)}, u32[]{:S(2)}, u32[]{:S(2)}) collective-permute-start(bf16[224,592]{0,1:T(8,128)(2,1)S(1)} %pad_maximum_fusion.2), channel_id=1, source_target_pairs={{0,32},{32,64},{64,96},{96,0},{1,33},{33,65},{65,97},{97,1},{2,34}... | collective-permute-start | bytes 795656 | tf_op jit(solution)/shard_map/ppermute | solution.py:23
  227.0 14.0 %collective-permute-start.71 = (bf16[224,592]{0,1:T(8,128)(2,1)S(1)}, bf16[224,592]{0,1:T(8,128)(2,1)S(1)}, u32[]{:S(2)}, u32[]{:S(2)}) collective-permute-start(bf16[224,592]{0,1:T(8,128)(2,1)S(1)} %pad_maximum_fusion.5), channel_id=1, source_target_pairs={{0,96},{32,0},{64,32},{96,64},{1,97},{33,1},{65,33},{97,65},{2,98}... | collective-permute-start | bytes 795656 | tf_op jit(solution)/shard_map/ppermute | solution.py:23
  228.5 17.1 %collective-permute-start.72 = (bf16[224,592]{0,1:T(8,128)(2,1)S(1)}, bf16[224,592]{0,1:T(8,128)(2,1)S(1)}, u32[]{:S(2)}, u32[]{:S(2)}) collective-permute-start(bf16[224,592]{0,1:T(8,128)(2,1)S(1)} %add_convert_fusion.1), channel_id=1, source_target_pairs={{0,128},{128,0},{1,129},{129,1},{2,130},{130,2},{3,131},{131,3},{4... | collective-permute-start | bytes 795656 | tf_op jit(solution)/shard_map/ppermute | solution.py:23
  (75 other events, 751.5 us)

commit v2 on v1

--- a/solution.py
+++ b/solution.py
@@ -263,7 +263,7 @@
     parts = teacher_parts(rows, teacher_gain, project_weight, positions)
     near_own = ring_pieces(near, "x", parts[0])
     near_first, near_last = (near_own[1], near_own[4]), (near_own[2], near_own[3])
-    parts = [after(p, *near_first) for p in parts]
+    parts = [after(p, *near_last) for p in parts]
     near_other = [near_across, *swapped(near_own[1:])]
     student_hidden, teacher_hidden = after(student_hidden, near), after(teacher_hidden, near)
     wide = student_hidden.astype(F32)

time: 252 us -> 256 us (1.016)
  starting transfers between devices: 111 us -> 114 us
  waiting for transfers between devices: 89.3 us -> 92.3 us
    ppermute x16, starting transfers between devices: 20.6 us -> 25.5 us  [exchange(): return lax.ppermute(array, axis, [(i, i ^ bits) for i in range(AXES[axis])])]
    ppermute x57, waiting for transfers between devices: 78.3 us -> 82.9 us  [shift(): lax.ppermute(array, axis, [(i, (i + by) % size) for i in range(size)])]
    unnamed x70 -> x64, local copies, waits for them, and re-layouts: 7.31 us -> 6.98 us
  transfers between devices with their start and end apart: 73 -> 73, of which waited for: 28 -> 29; matrix products, arithmetic and copies ran while one was open for 10% -> 9% of each run, Pallas kernels for 1% -> 1%
where the time goes in v2:
time: 256 us; the launch traced here: 252 us
  starting transfers between devices  114 us (45%)
  waiting for transfers between devices  92.3 us (36%)
  local copies, waits for them, and re-layouts  16.9 us (7%)
  Pallas kernels  12.9 us (5%)
  other arithmetic  9.63 us (4%)
  matrix products  3.52 us (1%)
    ppermute x57, starting transfers between devices, shift(): lax.ppermute(array, axis, [(i, (i + by) % size) for i in range(size)])  88.8 us
    ppermute x57, waiting for transfers between devices, shift(): lax.ppermute(array, axis, [(i, (i + by) % size) for i in range(size)])  82.9 us
    ppermute x16, starting transfers between devices, exchange(): return lax.ppermute(array, axis, [(i, i ^ bits) for i in range(AXES[axis])])  25.5 us
    pallas_call x1, Pallas kernels, feed_forward(): pl.pallas_call(kernel, grid=(1,), in_specs=[pl.BlockSpec(rows.shape, lamb...  11.3 us
    ppermute x16, waiting for transfers between devices, exchange(): return lax.ppermute(array, axis, [(i, i ^ bits) for i in range(AXES[axis])])  9.42 us
    unnamed x64, local copies, waits for them, and re-layouts  6.98 us
  transfers between devices with their start and end apart: 73, of which 29 were waited for; matrix products, arithmetic and copies ran while one was open for 9% of the time, Pallas kernels for 1%

profile of v2, /device:TPU:32, one launch (start us, length us, event | category | flops | bytes accessed | tf_op | source)
XLA Modules:
  0.0 251.7 jit_solution(3440404201621673944)
XLA Ops:
  5.6 6.3 %collective-permute-start = (bf16[224,1776]{1,0:T(8,128)(2,1)S(1)}, bf16[224,1776]{1,0:T(8,128)(2,1)}, u32[]{:S(2)}, u32[]{:S(2)}) collective-permute-start(bf16[224,1776]{1,0:T(8,128)(2,1)S(1)} %concatenate.94.refs_0_), channel_id=1, source_target_pairs={{0,128},{128,0},{1,129},{129,1},{2,130},{130,2},{3,131},{131,3},{4... | collective-permute-start | bytes 2386952 | tf_op jit(solution)/shard_map/ppermute | solution.py:23
  26.4 3.0 %collective-permute-start.7 = (bf16[112,1776]{1,0:T(8,128)(2,1)S(1)}, bf16[112,1776]{1,0:T(8,128)(2,1)}, u32[]{:S(2)}, u32[]{:S(2)}) collective-permute-start(bf16[112,1776]{1,0:T(8,128)(2,1)S(1)} %slice.272), channel_id=1, source_target_pairs={{0,96},{32,0},{64,32},{96,64},{1,97},{33,1},{65,33},{97,65},{2,98}... | collective-permute-start | bytes 1193480 | tf_op jit(solution)/shard_map/ppermute | solution.py:23
  29.4 7.8 %collective-permute-done.5.refs_2_ = bf16[112,1776]{1,0:T(8,128)(2,1)} collective-permute-done((bf16[112,1776]{1,0:T(8,128)(2,1)S(1)}, bf16[112,1776]{1,0:T(8,128)(2,1)}, u32[]{:S(2)}, u32[]{:S(2)}) %collective-permute-start.5) | collective-permute-done | bytes 397856 | tf_op jit(solution)/shard_map/ppermute | solution.py:23
  41.3 3.4 %collective-permute-done.23 = bf16[32,3584]{1,0:T(8,128)(2,1)S(1)} collective-permute-done((bf16[32,3584]{1,0:T(8,128)(2,1)S(1)}, bf16[32,3584]{1,0:T(8,128)(2,1)S(1)}, u32[]{:S(2)}, u32[]{:S(2)}) %collective-permute-start.23) | collective-permute-done | bytes 229408 | tf_op jit(solution)/shard_map/ppermute | solution.py:23
  57.0 3.2 %collective-permute-start.11 = (bf16[32,3712]{1,0:T(8,128)(2,1)S(1)}, bf16[32,3712]{1,0:T(8,128)(2,1)S(1)}, u32[]{:S(2)}, u32[]{:S(2)}) collective-permute-start(bf16[32,3712]{1,0:T(8,128)(2,1)S(1)} %get-tuple-element.122), channel_id=1, source_target_pairs={{0,8},{4,12},{8,0},{12,4},{1,9},{5,13},{9,1},{13,5},{2,10},{6,14},... | collective-permute-start | bytes 712712 | tf_op jit(solution)/shard_map/ppermute | solution.py:38
  64.1 16.9 %collective-permute-done.13.refs_14_ = bf16[224,1776]{1,0:T(8,128)(2,1)S(1)} collective-permute-done((bf16[224,1776]{1,0:T(8,128)(2,1)}, bf16[224,1776]{1,0:T(8,128)(2,1)S(1)}, u32[]{:S(2)}, u32[]{:S(2)}) %collective-permute-start.13) | collective-permute-done | bytes 795680 | tf_op jit(solution)/shard_map/ppermute | solution.py:23
  82.7 3.3 %collective-permute-start.18 = (bf16[112,1776]{1,0:T(8,128)(2,1)}, bf16[112,1776]{1,0:T(8,128)(2,1)}, u32[]{:S(2)}, u32[]{:S(2)}) collective-permute-start(bf16[112,1776]{1,0:T(8,128)(2,1)} %slice.275), channel_id=1, source_target_pairs={{0,96},{32,0},{64,32},{96,64},{1,97},{33,1},{65,33},{97,65},{2,98}... | collective-permute-start | bytes 1193480 | tf_op jit(solution)/shard_map/ppermute | solution.py:23
  96.0 3.5 %collective-permute-start.28 = (bf16[16,3584]{1,0:T(8,128)(2,1)S(1)}, bf16[16,3584]{1,0:T(8,128)(2,1)S(1)}, u32[]{:S(2)}, u32[]{:S(2)}) collective-permute-start(bf16[16,3584]{1,0:T(8,128)(2,1)S(1)} %slice.383), channel_id=1, source_target_pairs={{0,4},{4,0},{8,12},{12,8},{1,5},{5,1},{9,13},{13,9},{2,6},{6,2},{1... | collective-permute-start | bytes 344072 | tf_op jit(solution)/shard_map/ppermute | solution.py:38
  101.3 9.3 %collective-permute-start.21 = (bf16[32,3712]{1,0:T(8,128)(2,1)S(1)}, bf16[32,3712]{1,0:T(8,128)(2,1)S(1)}, u32[]{:S(2)}, u32[]{:S(2)}) collective-permute-start(bf16[32,3712]{1,0:T(8,128)(2,1)S(1)} %slice.273), channel_id=1, source_target_pairs={{0,1},{1,2},{2,3},{3,0},{4,5},{5,6},{6,7},{7,4},{8,9},{9,10},{10,1... | collective-permute-start | bytes 712712 | tf_op jit(solution)/shard_map/ppermute | solution.py:23
  110.6 3.0 %collective-permute-start.22 = (bf16[32,3712]{1,0:T(8,128)(2,1)S(1)}, bf16[32,3712]{1,0:T(8,128)(2,1)S(1)}, u32[]{:S(2)}, u32[]{:S(2)}) collective-permute-start(bf16[32,3712]{1,0:T(8,128)(2,1)S(1)} %slice.276), channel_id=1, source_target_pairs={{0,3},{1,0},{2,1},{3,2},{4,7},{5,4},{6,5},{7,6},{8,11},{9,8},{10,9... | collective-permute-start | bytes 712712 | tf_op jit(solution)/shard_map/ppermute | solution.py:23
  113.6 6.0 %collective-permute-done.21 = bf16[32,3712]{1,0:T(8,128)(2,1)S(1)} collective-permute-done((bf16[32,3712]{1,0:T(8,128)(2,1)S(1)}, bf16[32,3712]{1,0:T(8,128)(2,1)S(1)}, u32[]{:S(2)}, u32[]{:S(2)}) %collective-permute-start.21) | collective-permute-done | bytes 237600 | tf_op jit(solution)/shard_map/ppermute | solution.py:23
  121.1 11.3 %shard_map.132 = (bf16[256,592]{1,0:T(8,128)(2,1)}, bf16[64,1792]{1,0:T(8,128)(2,1)}, bf16[64,1792]{1,0:T(8,128)(2,1)}, bf16[64,1792]{1,0:T(8,128)(2,1)}, bf16[6...) custom-call(bf16[256,3712]{1,0:T(8,128)(2,1)} %copy-done.5, ...), custom_call_target="tpu_custom_call" | custom-call | tf_op jit(solution)/shard_map/pallas_call | solution.py:114
  132.5 4.5 %collective-permute-start.38 = (bf16[64,1792]{1,0:T(8,128)(2,1)}, bf16[64,1792]{1,0:T(8,128)(2,1)S(1)}, u32[]{:S(2)}, u32[]{:S(2)}) collective-permute-start(bf16[64,1792]{1,0:T(8,128)(2,1)} %get-tuple-element.70), channel_id=1, source_target_pairs={{0,2},{1,3},{2,0},{3,1},{4,6},{5,7},{6,4},{7,5},{8,10},{9,11},{10,... | collective-permute-start | bytes 688136 | tf_op jit(solution)/shard_map/ppermute | solution.py:23
  139.7 6.2 %collective-permute-done.37 = bf16[64,1792]{1,0:T(8,128)(2,1)S(1)} collective-permute-done((bf16[64,1792]{1,0:T(8,128)(2,1)}, bf16[64,1792]{1,0:T(8,128)(2,1)S(1)}, u32[]{:S(2)}, u32[]{:S(2)}) %collective-permute-start.37) | collective-permute-done | bytes 229408 | tf_op jit(solution)/shard_map/ppermute | solution.py:23
  153.3 3.5 %collective-permute-done.32 = bf16[64,1792]{1,0:T(8,128)(2,1)S(1)} collective-permute-done((bf16[64,1792]{1,0:T(8,128)(2,1)}, bf16[64,1792]{1,0:T(8,128)(2,1)S(1)}, u32[]{:S(2)}, u32[]{:S(2)}) %collective-permute-start.32) | collective-permute-done | bytes 229408 | tf_op jit(solution)/shard_map/ppermute | solution.py:23
  165.1 3.4 %collective-permute-start.57 = (bf16[16,1792]{1,0:T(8,128)(2,1)S(1)}, bf16[16,1792]{1,0:T(8,128)(2,1)S(1)}, u32[]{:S(2)}, u32[]{:S(2)}) collective-permute-start(bf16[16,1792]{1,0:T(8,128)(2,1)S(1)} %get-tuple-element.85), channel_id=1, source_target_pairs={{0,4},{4,0},{8,12},{12,8},{1,5},{5,1},{9,13},{13,9},{2,6},{6,2},{1... | collective-permute-start | bytes 172040 | tf_op jit(solution)/shard_map/ppermute | solution.py:38
  182.1 6.2 %collective-permute-done.61 = bf16[64,1792]{1,0:T(8,128)(2,1)S(1)} collective-permute-done((bf16[64,1792]{1,0:T(8,128)(2,1)S(1)}, bf16[64,1792]{1,0:T(8,128)(2,1)S(1)}, u32[]{:S(2)}, u32[]{:S(2)}) %collective-permute-start.61) | collective-permute-done | bytes 229408 | tf_op jit(solution)/shard_map/ppermute | solution.py:23
  188.4 3.5 %collective-permute-start.63 = (bf16[32,1792]{1,0:T(8,128)(2,1)S(1)}, bf16[32,1792]{1,0:T(8,128)(2,1)S(1)}, u32[]{:S(2)}, u32[]{:S(2)}) collective-permute-start(bf16[32,1792]{1,0:T(8,128)(2,1)S(1)} %slice.307), channel_id=1, source_target_pairs={{0,3},{1,0},{2,1},{3,2},{4,7},{5,4},{6,5},{7,6},{8,11},{9,8},{10,9... | collective-permute-start | bytes 344072 | tf_op jit(solution)/shard_map/ppermute | solution.py:23
  193.4 3.3 %collective-permute-start.50 = (bf16[32,1792]{1,0:T(8,128)(2,1)S(1)}, bf16[32,1792]{1,0:T(8,128)(2,1)S(1)}, u32[]{:S(2)}, u32[]{:S(2)}) collective-permute-start(bf16[32,1792]{1,0:T(8,128)(2,1)S(1)} %slice.297), channel_id=1, source_target_pairs={{0,3},{1,0},{2,1},{3,2},{4,7},{5,4},{6,5},{7,6},{8,11},{9,8},{10,9... | collective-permute-start | bytes 344072 | tf_op jit(solution)/shard_map/ppermute | solution.py:23
  203.5 3.2 %collective-permute-start.65 = (bf16[112,592]{0,1:T(8,128)(2,1)S(1)}, bf16[112,592]{0,1:T(8,128)(2,1)S(1)}, u32[]{:S(2)}, u32[]{:S(2)}) collective-permute-start(bf16[112,592]{0,1:T(8,128)(2,1)S(1)} %get-tuple-element.100), channel_id=1, source_target_pairs={{0,96},{32,0},{64,32},{96,64},{1,97},{33,1},{65,33},{97,65},{2,98}... | collective-permute-start | bytes 397832 | tf_op jit(solution)/shard_map/ppermute | solution.py:23
  207.4 3.3 %collective-permute-done.52 = bf16[112,592]{0,1:T(8,128)(2,1)S(1)} collective-permute-done((bf16[112,592]{0,1:T(8,128)(2,1)S(1)}, bf16[112,592]{0,1:T(8,128)(2,1)S(1)}, u32[]{:S(2)}, u32[]{:S(2)}) %collective-permute-start.52) | collective-permute-done | bytes 132640 | tf_op jit(solution)/shard_map/ppermute | solution.py:23
  212.6 4.9 %collective-permute-start.53 = (bf16[16,3584]{1,0:T(8,128)(2,1)S(1)}, bf16[16,3584]{1,0:T(8,128)(2,1)S(1)}, u32[]{:S(2)}, u32[]{:S(2)}) collective-permute-start(bf16[16,3584]{1,0:T(8,128)(2,1)S(1)} %pad_maximum_fusion.11), channel_id=1, source_target_pairs={{0,128},{128,0},{1,129},{129,1},{2,130},{130,2},{3,131},{131,3},{4... | collective-permute-start | bytes 344072 | tf_op jit(solution)/shard_map/ppermute | solution.py:23
  233.2 4.9 %collective-permute-start.72 = (bf16[224,592]{0,1:T(8,128)(2,1)S(1)}, bf16[224,592]{0,1:T(8,128)(2,1)S(1)}, u32[]{:S(2)}, u32[]{:S(2)}) collective-permute-start(bf16[224,592]{0,1:T(8,128)(2,1)S(1)} %add_convert_fusion.1), channel_id=1, source_target_pairs={{0,128},{128,0},{1,129},{129,1},{2,130},{130,2},{3,131},{131,3},{4... | collective-permute-start | bytes 795656 | tf_op jit(solution)/shard_map/ppermute | solution.py:23
  245.5 4.8 %collective-permute-done.72 = bf16[224,592]{0,1:T(8,128)(2,1)S(1)} collective-permute-done((bf16[224,592]{0,1:T(8,128)(2,1)S(1)}, bf16[224,592]{0,1:T(8,128)(2,1)S(1)}, u32[]{:S(2)}, u32[]{:S(2)}) %collective-permute-start.72) | collective-permute-done | bytes 265248 | tf_op jit(solution)/shard_map/ppermute | solution.py:23
  (288 shorter events, 121.1 us)
Async XLA Ops:
  2.2 14.8 %collective-permute-start.1 = (bf16[224,1776]{1,0:T(8,128)(2,1)S(1)}, bf16[224,1776]{1,0:T(8,128)(2,1)S(1)}, u32[]{:S(2)}, u32[]{:S(2)}) collective-permute-start(bf16[224,1776]{1,0:T(8,128)(2,1)S(1)} %concatenate.94.refs_0_), channel_id=1, source_target_pairs={{0,16},{16,0},{1,17},{17,1},{2,18},{18,2},{3,19},{19,3},{4,20},{20... | collective-permute-start | bytes 2386952 | tf_op jit(solution)/shard_map/ppermute | solution.py:23
  2.3 21.6 %collective-permute-start.4 = (bf16[224,1776]{1,0:T(8,128)(2,1)S(1)}, bf16[224,1776]{1,0:T(8,128)(2,1)}, u32[]{:S(2)}, u32[]{:S(2)}) collective-permute-start(bf16[224,1776]{1,0:T(8,128)(2,1)S(1)} %concatenate.94.refs_0_), channel_id=1, source_target_pairs={{0,32},{32,64},{64,96},{96,0},{1,33},{33,65},{65,97},{97,1},{2,34}... | collective-permute-start | bytes 2386952 | tf_op jit(solution)/shard_map/ppermute | solution.py:23
  3.9 21.4 %collective-permute-start.2 = (bf16[224,1776]{1,0:T(8,128)(2,1)S(1)}, bf16[224,1776]{1,0:T(8,128)(2,1)}, u32[]{:S(2)}, u32[]{:S(2)}) collective-permute-start(bf16[224,1776]{1,0:T(8,128)(2,1)S(1)} %concatenate.94.refs_0_), channel_id=1, source_target_pairs={{0,96},{32,0},{64,32},{96,64},{1,97},{33,1},{65,33},{97,65},{2,98}... | collective-permute-start | bytes 2386952 | tf_op jit(solution)/shard_map/ppermute | solution.py:23
  5.6 41.8 %collective-permute-start = (bf16[224,1776]{1,0:T(8,128)(2,1)S(1)}, bf16[224,1776]{1,0:T(8,128)(2,1)}, u32[]{:S(2)}, u32[]{:S(2)}) collective-permute-start(bf16[224,1776]{1,0:T(8,128)(2,1)S(1)} %concatenate.94.refs_0_), channel_id=1, source_target_pairs={{0,128},{128,0},{1,129},{129,1},{2,130},{130,2},{3,131},{131,3},{4... | collective-permute-start | bytes 2386952 | tf_op jit(solution)/shard_map/ppermute | solution.py:23
  47.4 16.5 %collective-permute-start.24 = (bf16[64,3584]{1,0:T(8,128)(2,1)S(1)}, bf16[64,3584]{1,0:T(8,128)(2,1)S(1)}, u32[]{:S(2)}, u32[]{:S(2)}) collective-permute-start(bf16[64,3584]{1,0:T(8,128)(2,1)S(1)} %pad_maximum_fusion), channel_id=1, source_target_pairs={{0,1},{1,2},{2,3},{3,0},{4,5},{5,6},{6,7},{7,4},{8,9},{9,10},{10,1... | collective-permute-start | bytes 1376264 | tf_op jit(solution)/shard_map/ppermute | solution.py:23
  49.3 14.6 %collective-permute-start.26 = (bf16[64,3584]{1,0:T(8,128)(2,1)S(1)}, bf16[64,3584]{1,0:T(8,128)(2,1)S(1)}, u32[]{:S(2)}, u32[]{:S(2)}) collective-permute-start(bf16[64,3584]{1,0:T(8,128)(2,1)S(1)} %pad_maximum_fusion.1), channel_id=1, source_target_pairs={{0,3},{1,0},{2,1},{3,2},{4,7},{5,4},{6,5},{7,6},{8,11},{9,8},{10,9... | collective-permute-start | bytes 1376264 | tf_op jit(solution)/shard_map/ppermute | solution.py:23
  57.0 29.0 %collective-permute-start.11 = (bf16[32,3712]{1,0:T(8,128)(2,1)S(1)}, bf16[32,3712]{1,0:T(8,128)(2,1)S(1)}, u32[]{:S(2)}, u32[]{:S(2)}) collective-permute-start(bf16[32,3712]{1,0:T(8,128)(2,1)S(1)} %get-tuple-element.122), channel_id=1, source_target_pairs={{0,8},{4,12},{8,0},{12,4},{1,9},{5,13},{9,1},{13,5},{2,10},{6,14},... | collective-permute-start | bytes 712712 | tf_op jit(solution)/shard_map/ppermute | solution.py:38
  60.1 20.9 %collective-permute-start.13 = (bf16[224,1776]{1,0:T(8,128)(2,1)}, bf16[224,1776]{1,0:T(8,128)(2,1)S(1)}, u32[]{:S(2)}, u32[]{:S(2)}) collective-permute-start(bf16[224,1776]{1,0:T(8,128)(2,1)} %collective-permute-done.refs_10_), channel_id=1, source_target_pairs={{0,32},{32,64},{64,96},{96,0},{1,33},{33,65},{65,97},{97,1},{2,34}... | collective-permute-start | bytes 2386952 | tf_op jit(solution)/shard_map/ppermute | solution.py:23
  61.2 20.6 %collective-permute-start.12 = (bf16[224,1776]{1,0:T(8,128)(2,1)}, bf16[224,1776]{1,0:T(8,128)(2,1)S(1)}, u32[]{:S(2)}, u32[]{:S(2)}) collective-permute-start(bf16[224,1776]{1,0:T(8,128)(2,1)} %collective-permute-done.refs_10_), channel_id=1, source_target_pairs={{0,96},{32,0},{64,32},{96,64},{1,97},{33,1},{65,33},{97,65},{2,98}... | collective-permute-start | bytes 2386952 | tf_op jit(solution)/shard_map/ppermute | solution.py:23
  63.9 24.1 %collective-permute-start.14 = (bf16[224,1776]{1,0:T(8,128)(2,1)}, bf16[224,1776]{1,0:T(8,128)(2,1)}, u32[]{:S(2)}, u32[]{:S(2)}) collective-permute-start(bf16[224,1776]{1,0:T(8,128)(2,1)} %collective-permute-done.refs_10_), channel_id=1, source_target_pairs={{0,16},{16,0},{1,17},{17,1},{2,18},{18,2},{3,19},{19,3},{4,20},{20... | collective-permute-start | bytes 2386952 | tf_op jit(solution)/shard_map/ppermute | solution.py:23
  96.0 24.0 %collective-permute-start.28 = (bf16[16,3584]{1,0:T(8,128)(2,1)S(1)}, bf16[16,3584]{1,0:T(8,128)(2,1)S(1)}, u32[]{:S(2)}, u32[]{:S(2)}) collective-permute-start(bf16[16,3584]{1,0:T(8,128)(2,1)S(1)} %slice.383), channel_id=1, source_target_pairs={{0,4},{4,0},{8,12},{12,8},{1,5},{5,1},{9,13},{13,9},{2,6},{6,2},{1... | collective-permute-start | bytes 344072 | tf_op jit(solution)/shard_map/ppermute | solution.py:38
  100.5 19.6 %collective-permute-start.29 = (bf16[112,1776]{1,0:T(8,128)(2,1)S(1)}, bf16[112,1776]{1,0:T(8,128)(2,1)S(1)}, u32[]{:S(2)}, u32[]{:S(2)}) collective-permute-start(bf16[112,1776]{1,0:T(8,128)(2,1)S(1)} %copy-done.16), channel_id=1, source_target_pairs={{0,16},{16,0},{1,17},{17,1},{2,18},{18,2},{3,19},{19,3},{4,20},{20... | collective-permute-start | bytes 1193480 | tf_op jit(solution)/shard_map/ppermute | solution.py:23
  101.2 19.9 %collective-permute-start.30 = (bf16[112,1776]{1,0:T(8,128)(2,1)}, bf16[112,1776]{1,0:T(8,128)(2,1)}, u32[]{:S(2)}, u32[]{:S(2)}) collective-permute-start(bf16[112,1776]{1,0:T(8,128)(2,1)} %collective-permute-done.18.refs_13_), channel_id=1, source_target_pairs={{0,16},{16,0},{1,17},{17,1},{2,18},{18,2},{3,19},{19,3},{4,20},{20... | collective-permute-start | bytes 1193480 | tf_op jit(solution)/shard_map/ppermute | solution.py:23
  101.3 18.3 %collective-permute-start.21 = (bf16[32,3712]{1,0:T(8,128)(2,1)S(1)}, bf16[32,3712]{1,0:T(8,128)(2,1)S(1)}, u32[]{:S(2)}, u32[]{:S(2)}) collective-permute-start(bf16[32,3712]{1,0:T(8,128)(2,1)S(1)} %slice.273), channel_id=1, source_target_pairs={{0,1},{1,2},{2,3},{3,0},{4,5},{5,6},{6,7},{7,4},{8,9},{9,10},{10,1... | collective-permute-start | bytes 712712 | tf_op jit(solution)/shard_map/ppermute | solution.py:23
  132.5 16.2 %collective-permute-start.38 = (bf16[64,1792]{1,0:T(8,128)(2,1)}, bf16[64,1792]{1,0:T(8,128)(2,1)S(1)}, u32[]{:S(2)}, u32[]{:S(2)}) collective-permute-start(bf16[64,1792]{1,0:T(8,128)(2,1)} %get-tuple-element.70), channel_id=1, source_target_pairs={{0,2},{1,3},{2,0},{3,1},{4,6},{5,7},{6,4},{7,5},{8,10},{9,11},{10,... | collective-permute-start | bytes 688136 | tf_op jit(solution)/shard_map/ppermute | solution.py:23
  137.0 15.9 %collective-permute-start.31 = (bf16[64,1792]{1,0:T(8,128)(2,1)}, bf16[64,1792]{1,0:T(8,128)(2,1)S(1)}, u32[]{:S(2)}, u32[]{:S(2)}) collective-permute-start(bf16[64,1792]{1,0:T(8,128)(2,1)} %get-tuple-element.65), channel_id=1, source_target_pairs={{0,1},{1,2},{2,3},{3,0},{4,5},{5,6},{6,7},{7,4},{8,9},{9,10},{10,1... | collective-permute-start | bytes 688136 | tf_op jit(solution)/shard_map/ppermute | solution.py:23
  139.0 17.9 %collective-permute-start.32 = (bf16[64,1792]{1,0:T(8,128)(2,1)}, bf16[64,1792]{1,0:T(8,128)(2,1)S(1)}, u32[]{:S(2)}, u32[]{:S(2)}) collective-permute-start(bf16[64,1792]{1,0:T(8,128)(2,1)} %get-tuple-element.66), channel_id=1, source_target_pairs={{0,2},{1,3},{2,0},{3,1},{4,6},{5,7},{6,4},{7,5},{8,10},{9,11},{10,... | collective-permute-start | bytes 688136 | tf_op jit(solution)/shard_map/ppermute | solution.py:23
  176.8 23.3 %collective-permute-start.43 = (bf16[16,3584]{1,0:T(8,128)(2,1)S(1)}, bf16[16,3584]{1,0:T(8,128)(2,1)S(1)}, u32[]{:S(2)}, u32[]{:S(2)}) collective-permute-start(bf16[16,3584]{1,0:T(8,128)(2,1)S(1)} %convolution_convert_fusion.2), channel_id=1, source_target_pairs={{0,16},{16,0},{1,17},{17,1},{2,18},{18,2},{3,19},{19,3},{4,20},{20... | collective-permute-start | bytes 344072 | tf_op jit(solution)/shard_map/ppermute | solution.py:23
  179.5 13.8 %collective-permute-start.47 = (bf16[64,1792]{1,0:T(8,128)(2,1)S(1)}, bf16[64,1792]{1,0:T(8,128)(2,1)S(1)}, u32[]{:S(2)}, u32[]{:S(2)}) collective-permute-start(bf16[64,1792]{1,0:T(8,128)(2,1)S(1)} %pad_maximum_fusion.7), channel_id=1, source_target_pairs={{0,3},{1,0},{2,1},{3,2},{4,7},{5,4},{6,5},{7,6},{8,11},{9,8},{10,9... | collective-permute-start | bytes 688136 | tf_op jit(solution)/shard_map/ppermute | solution.py:23
  211.1 18.6 %collective-permute-start.67 = (bf16[224,592]{0,1:T(8,128)(2,1)S(1)}, bf16[224,592]{0,1:T(8,128)(2,1)S(1)}, u32[]{:S(2)}, u32[]{:S(2)}) collective-permute-start(bf16[224,592]{0,1:T(8,128)(2,1)S(1)} %pad_maximum_fusion.3), channel_id=1, source_target_pairs={{0,32},{32,64},{64,96},{96,0},{1,33},{33,65},{65,97},{97,1},{2,34}... | collective-permute-start | bytes 795656 | tf_op jit(solution)/shard_map/ppermute | solution.py:23
  225.0 15.2 %collective-permute-start.54 = (bf16[8,3584]{1,0:T(8,128)(2,1)S(1)}, bf16[8,3584]{1,0:T(8,128)(2,1)S(1)}, u32[]{:S(2)}, u32[]{:S(2)}) collective-permute-start(bf16[8,3584]{1,0:T(8,128)(2,1)S(1)} %get-tuple-element.113), channel_id=1, source_target_pairs={{0,32},{32,64},{64,96},{96,0},{1,33},{33,65},{65,97},{97,1},{2,34}... | collective-permute-start | bytes 172040 | tf_op jit(solution)/shard_map/ppermute | solution.py:23
  229.9 15.6 %collective-permute-start.69 = (bf16[224,592]{0,1:T(8,128)(2,1)S(1)}, bf16[224,592]{0,1:T(8,128)(2,1)S(1)}, u32[]{:S(2)}, u32[]{:S(2)}) collective-permute-start(bf16[224,592]{0,1:T(8,128)(2,1)S(1)} %pad_maximum_fusion.2), channel_id=1, source_target_pairs={{0,32},{32,64},{64,96},{96,0},{1,33},{33,65},{65,97},{97,1},{2,34}... | collective-permute-start | bytes 795656 | tf_op jit(solution)/shard_map/ppermute | solution.py:23
  231.7 13.8 %collective-permute-start.71 = (bf16[224,592]{0,1:T(8,128)(2,1)S(1)}, bf16[224,592]{0,1:T(8,128)(2,1)S(1)}, u32[]{:S(2)}, u32[]{:S(2)}) collective-permute-start(bf16[224,592]{0,1:T(8,128)(2,1)S(1)} %pad_maximum_fusion.5), channel_id=1, source_target_pairs={{0,96},{32,0},{64,32},{96,64},{1,97},{33,1},{65,33},{97,65},{2,98}... | collective-permute-start | bytes 795656 | tf_op jit(solution)/shard_map/ppermute | solution.py:23
  233.2 17.1 %collective-permute-start.72 = (bf16[224,592]{0,1:T(8,128)(2,1)S(1)}, bf16[224,592]{0,1:T(8,128)(2,1)S(1)}, u32[]{:S(2)}, u32[]{:S(2)}) collective-permute-start(bf16[224,592]{0,1:T(8,128)(2,1)S(1)} %add_convert_fusion.1), channel_id=1, source_target_pairs={{0,128},{128,0},{1,129},{129,1},{2,130},{130,2},{3,131},{131,3},{4... | collective-permute-start | bytes 795656 | tf_op jit(solution)/shard_map/ppermute | solution.py:23
  (72 other events, 706.9 us)
